TPU v7x, 512 devices: a whole 4x8x8 slice. The times are simulated.
512 devices in a mesh: blk: 64 (over y_lo, z, x), rep: 8 (over y_hi, core).
Axes of the slice: x: 4, y: 8 (y_hi: 4, y_lo: 2; y = y_hi * 2 + y_lo), z: 8, core: 2. Of those that a mesh axis runs over, the one named last changes fastest.
Arguments:
- features: bfloat16 [524288, 256], P(('blk', 'rep')), may hold values from -6 to 6
- block_cols: int32 [4096, 44], P(('blk', 'rep')), may hold values from 0 to 4095, as said below
- adjacency: int32 [4096, 44, 4, 128], P(('blk', 'rep')), may hold values from 0 to 511, as said below
- w_self: bfloat16 [256, 256], replicated, may hold values from -0.375 to 0.375
- w_neigh: bfloat16 [256, 256], replicated, may hold values from -0.375 to 0.375
- bias: float32 [256], replicated, may hold values from -4 to 4
Outputs:
- mixed: bfloat16 [524288, 256], P(('blk', 'rep'))
Inputs may be any that keep to these rules, and one draw needn't show every extreme that they name: `block_cols`: the 44 numbers of a block row b are different, and each lies in the group of block b or in the group just before or after it on a closed loop of groups, group of block c being c // 64. `adjacency`: each entry is 4 times a column within the block plus an edge count of 0 to 3.
All inputs are finite; a program needn't handle non-finite values.
Results may differ from a plain program's by a relative error of at most 0.0021.
Values may be sent and summed in bfloat16 or wider, within the bound.
No kernel may reach another device: no remote copies, remote signals or barrier semaphores. Data moves between devices by JAX's collectives and lax.ppermute only.
A program may use at most 128 MiB of HBM per device.

v0:
```python
import jax
import jax.numpy as jnp
from jax import lax
from jax.sharding import PartitionSpec as P

BS = 128


def with_halo(value, sides, width):
    for axis, dim in sides:
        devices, length = (lax.axis_size(axis), value.shape[dim])
        up = [(i, (i + 1) % devices) for i in range(devices)]
        down = [(j, i) for i, j in up]
        last = lax.slice_in_dim(value, length - width, length, axis=dim)
        leading = lax.slice_in_dim(value, 0, width, axis=dim)
        before = lax.ppermute(last, axis, up)
        after = lax.ppermute(leading, axis, down)
        value = jnp.concatenate([before, value, after], axis=dim)
    return value


def unpack_counts(words):
    columns = jnp.right_shift(words, 2)
    values = jnp.bitwise_and(words, 3)
    slots, edges, rows = words.shape
    places = jnp.arange(rows, dtype=jnp.int32)
    counts = jnp.zeros((slots, rows, rows), jnp.int32)
    for edge in range(edges):
        match = columns[:, edge, :, None] == places[None, None, :]
        counts = counts + jnp.where(match, values[:, edge, :, None], 0)
    counts = jnp.transpose(counts, (1, 0, 2)).reshape(rows, slots * rows)
    return counts


def shards(features, block_cols, adjacency, w_self, w_neigh, bias):
    node_dev, width = features.shape
    group_size = lax.axis_size("rep")
    loop_size = lax.axis_size("blk")
    group_blocks = node_dev // BS * group_size
    grouped = lax.all_gather(features, "rep", axis=0, tiled=True)
    window = with_halo(grouped, (("blk", 0),), grouped.shape[0])
    blocks = window.reshape(3 * group_blocks, BS, width)
    mine = lax.axis_index("blk")
    local_cols = (block_cols // group_blocks - mine + 1 + loop_size) % loop_size * group_blocks
    local_cols = local_cols + block_cols % group_blocks

    def one_row(pair):
        cols, words = pair
        counts = unpack_counts(words)
        gathered = jnp.take(blocks, cols, axis=0).reshape(-1, width)
        summed = jnp.dot(counts.astype(jnp.bfloat16), gathered, preferred_element_type=jnp.float32)
        degree = jnp.sum(counts.astype(jnp.float32), axis=1)
        return (summed, degree)

    summed, degree = lax.map(one_row, (local_cols, adjacency))
    summed = summed.reshape(node_dev, width)
    degree = degree.reshape(node_dev, 1)
    neighbour_mean = (summed / jnp.maximum(degree, jnp.float32(1.0))).astype(jnp.bfloat16)
    total = jnp.dot(features, w_self, preferred_element_type=jnp.float32)
    total = total + jnp.dot(neighbour_mean, w_neigh, preferred_element_type=jnp.float32) + bias
    return jnp.maximum(total, 0.0).astype(jnp.bfloat16)


def solution(mesh):
    in_specs = (
        P(("blk", "rep"), None),
        P(("blk", "rep"), None),
        P(("blk", "rep"), None, None, None),
        P(),
        P(),
        P(),
    )
    out_specs = P(("blk", "rep"), None)
    return jax.shard_map(shards, mesh=mesh, in_specs=in_specs, out_specs=out_specs, check_vma=False)
```

profile of v0, /device:TPU:1, one launch (start us, length us, event | category | flops | bytes accessed | tf_op | source)
XLA Modules:
  0.0 363.7 jit_solution(8693589763999751182)
XLA Ops:
  6.5 0.0 copy-start
  6.5 0.0 all-gather.2.cloned.1.call-start
  6.5 0.7 all-gather.2.cloned.1.call-update
  7.3 61.8 %all-gather.2.cloned.1.call-done = bf16[8192,256]{1,0:T(8,128)(2,1)} async-done(((bf16[1024,256]{1,0:T(8,128)(2,1)}), bf16[8192,256]{1,0:T(8,128)(2,1)}) %all-gather.2.cloned.1.call-update) | async-done | bytes 4194320 | tf_op jit(solution)/shard_map/all_gather | solution.py:40
  69.0 1.9 collective-permute-start
  71.0 10.2 %collective-permute-start.1 = (bf16[8192,256]{1,0:T(8,128)(2,1)}, bf16[8192,256]{1,0:T(8,128)(2,1)}, u32[]{:S(2)}, u32[]{:S(2)}) collective-permute-start(bf16[8192,256]{1,0:T(8,128)(2,1)} %all-gather.2.cloned.1.call-done), channel_id=1, source_target_pairs={{8,0},{16,8},{24,16},{32,24},{40,32},{48,40},{56,48},{64,56},{72,6... | collective-permute-start | bytes 12582920 | tf_op jit(solution)/shard_map/ppermute | solution.py:17
  81.2 0.7 fusion.36
  81.9 0.0 copy-done
  81.9 2.4 fusion.38
  84.3 86.0 %collective-permute-done = bf16[8192,256]{1,0:T(8,128)(2,1)} collective-permute-done((bf16[8192,256]{1,0:T(8,128)(2,1)}, bf16[8192,256]{1,0:T(8,128)(2,1)}, u32[]{:S(2)}, u32[]{:S(2)}) %collective-permute-start) | collective-permute-done | bytes 4194336 | tf_op jit(solution)/shard_map/ppermute | solution.py:16
  170.3 0.9 collective-permute-done.1
  171.1 15.4 %pad_maximum_fusion = bf16[24576,256]{1,0:T(8,128)(2,1)} fusion(bf16[8192,256]{1,0:T(8,128)(2,1)} %collective-permute-done.1, bf16[8192,256]{1,0:T(8,128)(2,1)} %all-gather.2.cloned.1.call-done, bf16[8192,256]{1,0:T(8,128)(2,1)} %collective-permute-done), kind=kLoop, calls=%fused_computation.42 | loop fusion | flops 37748736 | bytes 25165824 | tf_op jit(solution)/shard_map/concatenate | solution.py:18
  186.5 166.6 %while.12 = (s32[]{:T(128)}, f32[8,128,256]{2,1,0:T(8,128)}, f32[8,128]{1,0:T(8,128)S(1)}, s32[8,44,4,128]{3,2,1,0:T(4,128)}, s32[8,44]{1,0:T(8,128)S(1)}, /*ind...) while((s32[]{:T(128)}, f32[8,128,256]{2,1,0:T(8,128)}, f32[8,128]{1,0:T(8,128)S(1)}, ...), condition=%wide.region_2.3_spmd, body=%wide.region_0.2_spmd.sunk | while | flops 388609280 | bytes 9960493 | solution.py:55
  186.5 0.9 constant_dynamic-slice_fusion.3
  187.5 7.6 %convert_reduce_fusion.2 = f32[128]{0:T(128)S(1)} fusion(s32[128,44]{0,1:T(8,128)S(1)} %get-tuple-element.121, s32[128,44]{0,1:T(8,128)S(1)} %get-tuple-element.122, s32[128,44]{0,1:T(8,128)S(1)} %get-tuple-element.123, s32[128,44]{0,1:T(8,128)S(1)} %get-tuple-element.124, s32[128,44]{0,1:T(8,128)S(1)} %get-tuple-element.125, ...), kind=kLoop, calls=%fused_computation.1.clone.1 | loop fusion | flops 9371520 | bytes 180736 | tf_op jit(solution)/shard_map/while/body/eval_jaxpr/reduce_sum | solution.py:52
  195.2 5.3 %gather_fusion = bf16[44,128,256]{2,1,0:T(8,128)(2,1)S(1)} fusion(bf16[192,128,256]{2,1,0:T(8,128)(2,1)} %get-tuple-element.150, s32[1024]{0:T(1024)S(1)} %pad_clamp_fusion.2), kind=kCustom, calls=%fused_computation.clone.1 | custom fusion | bytes 5767344 | tf_op jit(solution)/shard_map/while/body/eval_jaxpr/jit(_take)/gather | solution.py:50
  200.5 6.9 %fusion.50 = f32[8,128,256]{2,1,0:T(8,128)} fusion(f32[8,128,256]{2,1,0:T(8,128)} %get-tuple-element.138, s32[]{:T(128)} %get-tuple-element.137, bf16[44,128,256]{2,1,0:T(8,128)(2,1)S(1)} %gather_fusion, pred[44]{0:T(512)(128)(4,1)S(1)} %compare_and_fusion.2, s32[128,44]{0,1:T(8,128)S(1)} %get-tuple-element.121, ...), kind=kOutput, calls=%fused_computation.22.clone.1 | convolution fusion | flops 379191296 | bytes 3195436 | tf_op jit(solution)/shard_map/while/body/eval_jaxpr/dot_general | solution.py:51
  207.4 0.9 constant_dynamic-slice_fusion.3
  208.3 7.6 %convert_reduce_fusion.2 = f32[128]{0:T(128)S(1)} fusion(s32[128,44]{0,1:T(8,128)S(1)} %get-tuple-element.121, s32[128,44]{0,1:T(8,128)S(1)} %get-tuple-element.122, s32[128,44]{0,1:T(8,128)S(1)} %get-tuple-element.123, s32[128,44]{0,1:T(8,128)S(1)} %get-tuple-element.124, s32[128,44]{0,1:T(8,128)S(1)} %get-tuple-element.125, ...), kind=kLoop, calls=%fused_computation.1.clone.1 | loop fusion | flops 9371520 | bytes 180736 | tf_op jit(solution)/shard_map/while/body/eval_jaxpr/reduce_sum | solution.py:52
  216.0 5.3 %gather_fusion = bf16[44,128,256]{2,1,0:T(8,128)(2,1)S(1)} fusion(bf16[192,128,256]{2,1,0:T(8,128)(2,1)} %get-tuple-element.150, s32[1024]{0:T(1024)S(1)} %pad_clamp_fusion.2), kind=kCustom, calls=%fused_computation.clone.1 | custom fusion | bytes 5767344 | tf_op jit(solution)/shard_map/while/body/eval_jaxpr/jit(_take)/gather | solution.py:50
  221.3 6.8 %fusion.50 = f32[8,128,256]{2,1,0:T(8,128)} fusion(f32[8,128,256]{2,1,0:T(8,128)} %get-tuple-element.138, s32[]{:T(128)} %get-tuple-element.137, bf16[44,128,256]{2,1,0:T(8,128)(2,1)S(1)} %gather_fusion, pred[44]{0:T(512)(128)(4,1)S(1)} %compare_and_fusion.2, s32[128,44]{0,1:T(8,128)S(1)} %get-tuple-element.121, ...), kind=kOutput, calls=%fused_computation.22.clone.1 | convolution fusion | flops 379191296 | bytes 3195436 | tf_op jit(solution)/shard_map/while/body/eval_jaxpr/dot_general | solution.py:51
  228.2 0.9 constant_dynamic-slice_fusion.3
  229.1 7.6 %convert_reduce_fusion.2 = f32[128]{0:T(128)S(1)} fusion(s32[128,44]{0,1:T(8,128)S(1)} %get-tuple-element.121, s32[128,44]{0,1:T(8,128)S(1)} %get-tuple-element.122, s32[128,44]{0,1:T(8,128)S(1)} %get-tuple-element.123, s32[128,44]{0,1:T(8,128)S(1)} %get-tuple-element.124, s32[128,44]{0,1:T(8,128)S(1)} %get-tuple-element.125, ...), kind=kLoop, calls=%fused_computation.1.clone.1 | loop fusion | flops 9371520 | bytes 180736 | tf_op jit(solution)/shard_map/while/body/eval_jaxpr/reduce_sum | solution.py:52
  236.8 5.3 %gather_fusion = bf16[44,128,256]{2,1,0:T(8,128)(2,1)S(1)} fusion(bf16[192,128,256]{2,1,0:T(8,128)(2,1)} %get-tuple-element.150, s32[1024]{0:T(1024)S(1)} %pad_clamp_fusion.2), kind=kCustom, calls=%fused_computation.clone.1 | custom fusion | bytes 5767344 | tf_op jit(solution)/shard_map/while/body/eval_jaxpr/jit(_take)/gather | solution.py:50
  242.2 6.9 %fusion.50 = f32[8,128,256]{2,1,0:T(8,128)} fusion(f32[8,128,256]{2,1,0:T(8,128)} %get-tuple-element.138, s32[]{:T(128)} %get-tuple-element.137, bf16[44,128,256]{2,1,0:T(8,128)(2,1)S(1)} %gather_fusion, pred[44]{0:T(512)(128)(4,1)S(1)} %compare_and_fusion.2, s32[128,44]{0,1:T(8,128)S(1)} %get-tuple-element.121, ...), kind=kOutput, calls=%fused_computation.22.clone.1 | convolution fusion | flops 379191296 | bytes 3195436 | tf_op jit(solution)/shard_map/while/body/eval_jaxpr/dot_general | solution.py:51
  249.0 0.9 constant_dynamic-slice_fusion.3
  250.0 7.6 %convert_reduce_fusion.2 = f32[128]{0:T(128)S(1)} fusion(s32[128,44]{0,1:T(8,128)S(1)} %get-tuple-element.121, s32[128,44]{0,1:T(8,128)S(1)} %get-tuple-element.122, s32[128,44]{0,1:T(8,128)S(1)} %get-tuple-element.123, s32[128,44]{0,1:T(8,128)S(1)} %get-tuple-element.124, s32[128,44]{0,1:T(8,128)S(1)} %get-tuple-element.125, ...), kind=kLoop, calls=%fused_computation.1.clone.1 | loop fusion | flops 9371520 | bytes 180736 | tf_op jit(solution)/shard_map/while/body/eval_jaxpr/reduce_sum | solution.py:52
  257.6 5.3 %gather_fusion = bf16[44,128,256]{2,1,0:T(8,128)(2,1)S(1)} fusion(bf16[192,128,256]{2,1,0:T(8,128)(2,1)} %get-tuple-element.150, s32[1024]{0:T(1024)S(1)} %pad_clamp_fusion.2), kind=kCustom, calls=%fused_computation.clone.1 | custom fusion | bytes 5767344 | tf_op jit(solution)/shard_map/while/body/eval_jaxpr/jit(_take)/gather | solution.py:50
  263.0 6.8 %fusion.50 = f32[8,128,256]{2,1,0:T(8,128)} fusion(f32[8,128,256]{2,1,0:T(8,128)} %get-tuple-element.138, s32[]{:T(128)} %get-tuple-element.137, bf16[44,128,256]{2,1,0:T(8,128)(2,1)S(1)} %gather_fusion, pred[44]{0:T(512)(128)(4,1)S(1)} %compare_and_fusion.2, s32[128,44]{0,1:T(8,128)S(1)} %get-tuple-element.121, ...), kind=kOutput, calls=%fused_computation.22.clone.1 | convolution fusion | flops 379191296 | bytes 3195436 | tf_op jit(solution)/shard_map/while/body/eval_jaxpr/dot_general | solution.py:51
  269.8 0.9 constant_dynamic-slice_fusion.3
  270.8 7.6 %convert_reduce_fusion.2 = f32[128]{0:T(128)S(1)} fusion(s32[128,44]{0,1:T(8,128)S(1)} %get-tuple-element.121, s32[128,44]{0,1:T(8,128)S(1)} %get-tuple-element.122, s32[128,44]{0,1:T(8,128)S(1)} %get-tuple-element.123, s32[128,44]{0,1:T(8,128)S(1)} %get-tuple-element.124, s32[128,44]{0,1:T(8,128)S(1)} %get-tuple-element.125, ...), kind=kLoop, calls=%fused_computation.1.clone.1 | loop fusion | flops 9371520 | bytes 180736 | tf_op jit(solution)/shard_map/while/body/eval_jaxpr/reduce_sum | solution.py:52
  278.5 5.3 %gather_fusion = bf16[44,128,256]{2,1,0:T(8,128)(2,1)S(1)} fusion(bf16[192,128,256]{2,1,0:T(8,128)(2,1)} %get-tuple-element.150, s32[1024]{0:T(1024)S(1)} %pad_clamp_fusion.2), kind=kCustom, calls=%fused_computation.clone.1 | custom fusion | bytes 5767344 | tf_op jit(solution)/shard_map/while/body/eval_jaxpr/jit(_take)/gather | solution.py:50
  283.8 6.8 %fusion.50 = f32[8,128,256]{2,1,0:T(8,128)} fusion(f32[8,128,256]{2,1,0:T(8,128)} %get-tuple-element.138, s32[]{:T(128)} %get-tuple-element.137, bf16[44,128,256]{2,1,0:T(8,128)(2,1)S(1)} %gather_fusion, pred[44]{0:T(512)(128)(4,1)S(1)} %compare_and_fusion.2, s32[128,44]{0,1:T(8,128)S(1)} %get-tuple-element.121, ...), kind=kOutput, calls=%fused_computation.22.clone.1 | convolution fusion | flops 379191296 | bytes 3195436 | tf_op jit(solution)/shard_map/while/body/eval_jaxpr/dot_general | solution.py:51
  290.6 0.9 constant_dynamic-slice_fusion.3
  291.6 7.6 %convert_reduce_fusion.2 = f32[128]{0:T(128)S(1)} fusion(s32[128,44]{0,1:T(8,128)S(1)} %get-tuple-element.121, s32[128,44]{0,1:T(8,128)S(1)} %get-tuple-element.122, s32[128,44]{0,1:T(8,128)S(1)} %get-tuple-element.123, s32[128,44]{0,1:T(8,128)S(1)} %get-tuple-element.124, s32[128,44]{0,1:T(8,128)S(1)} %get-tuple-element.125, ...), kind=kLoop, calls=%fused_computation.1.clone.1 | loop fusion | flops 9371520 | bytes 180736 | tf_op jit(solution)/shard_map/while/body/eval_jaxpr/reduce_sum | solution.py:52
  299.3 5.3 %gather_fusion = bf16[44,128,256]{2,1,0:T(8,128)(2,1)S(1)} fusion(bf16[192,128,256]{2,1,0:T(8,128)(2,1)} %get-tuple-element.150, s32[1024]{0:T(1024)S(1)} %pad_clamp_fusion.2), kind=kCustom, calls=%fused_computation.clone.1 | custom fusion | bytes 5767344 | tf_op jit(solution)/shard_map/while/body/eval_jaxpr/jit(_take)/gather | solution.py:50
  304.6 6.8 %fusion.50 = f32[8,128,256]{2,1,0:T(8,128)} fusion(f32[8,128,256]{2,1,0:T(8,128)} %get-tuple-element.138, s32[]{:T(128)} %get-tuple-element.137, bf16[44,128,256]{2,1,0:T(8,128)(2,1)S(1)} %gather_fusion, pred[44]{0:T(512)(128)(4,1)S(1)} %compare_and_fusion.2, s32[128,44]{0,1:T(8,128)S(1)} %get-tuple-element.121, ...), kind=kOutput, calls=%fused_computation.22.clone.1 | convolution fusion | flops 379191296 | bytes 3195436 | tf_op jit(solution)/shard_map/while/body/eval_jaxpr/dot_general | solution.py:51
  311.5 0.9 constant_dynamic-slice_fusion.3
  312.4 7.6 %convert_reduce_fusion.2 = f32[128]{0:T(128)S(1)} fusion(s32[128,44]{0,1:T(8,128)S(1)} %get-tuple-element.121, s32[128,44]{0,1:T(8,128)S(1)} %get-tuple-element.122, s32[128,44]{0,1:T(8,128)S(1)} %get-tuple-element.123, s32[128,44]{0,1:T(8,128)S(1)} %get-tuple-element.124, s32[128,44]{0,1:T(8,128)S(1)} %get-tuple-element.125, ...), kind=kLoop, calls=%fused_computation.1.clone.1 | loop fusion | flops 9371520 | bytes 180736 | tf_op jit(solution)/shard_map/while/body/eval_jaxpr/reduce_sum | solution.py:52
  320.1 5.3 %gather_fusion = bf16[44,128,256]{2,1,0:T(8,128)(2,1)S(1)} fusion(bf16[192,128,256]{2,1,0:T(8,128)(2,1)} %get-tuple-element.150, s32[1024]{0:T(1024)S(1)} %pad_clamp_fusion.2), kind=kCustom, calls=%fused_computation.clone.1 | custom fusion | bytes 5767344 | tf_op jit(solution)/shard_map/while/body/eval_jaxpr/jit(_take)/gather | solution.py:50
  325.4 6.8 %fusion.50 = f32[8,128,256]{2,1,0:T(8,128)} fusion(f32[8,128,256]{2,1,0:T(8,128)} %get-tuple-element.138, s32[]{:T(128)} %get-tuple-element.137, bf16[44,128,256]{2,1,0:T(8,128)(2,1)S(1)} %gather_fusion, pred[44]{0:T(512)(128)(4,1)S(1)} %compare_and_fusion.2, s32[128,44]{0,1:T(8,128)S(1)} %get-tuple-element.121, ...), kind=kOutput, calls=%fused_computation.22.clone.1 | convolution fusion | flops 379191296 | bytes 3195436 | tf_op jit(solution)/shard_map/while/body/eval_jaxpr/dot_general | solution.py:51
  332.3 0.9 constant_dynamic-slice_fusion.3
  333.2 7.6 %convert_reduce_fusion.2 = f32[128]{0:T(128)S(1)} fusion(s32[128,44]{0,1:T(8,128)S(1)} %get-tuple-element.121, s32[128,44]{0,1:T(8,128)S(1)} %get-tuple-element.122, s32[128,44]{0,1:T(8,128)S(1)} %get-tuple-element.123, s32[128,44]{0,1:T(8,128)S(1)} %get-tuple-element.124, s32[128,44]{0,1:T(8,128)S(1)} %get-tuple-element.125, ...), kind=kLoop, calls=%fused_computation.1.clone.1 | loop fusion | flops 9371520 | bytes 180736 | tf_op jit(solution)/shard_map/while/body/eval_jaxpr/reduce_sum | solution.py:52
  340.9 5.3 %gather_fusion = bf16[44,128,256]{2,1,0:T(8,128)(2,1)S(1)} fusion(bf16[192,128,256]{2,1,0:T(8,128)(2,1)} %get-tuple-element.150, s32[1024]{0:T(1024)S(1)} %pad_clamp_fusion.2), kind=kCustom, calls=%fused_computation.clone.1 | custom fusion | bytes 5767344 | tf_op jit(solution)/shard_map/while/body/eval_jaxpr/jit(_take)/gather | solution.py:50
  346.2 6.9 %fusion.50 = f32[8,128,256]{2,1,0:T(8,128)} fusion(f32[8,128,256]{2,1,0:T(8,128)} %get-tuple-element.138, s32[]{:T(128)} %get-tuple-element.137, bf16[44,128,256]{2,1,0:T(8,128)(2,1)S(1)} %gather_fusion, pred[44]{0:T(512)(128)(4,1)S(1)} %compare_and_fusion.2, s32[128,44]{0,1:T(8,128)S(1)} %get-tuple-element.121, ...), kind=kOutput, calls=%fused_computation.22.clone.1 | convolution fusion | flops 379191296 | bytes 3195436 | tf_op jit(solution)/shard_map/while/body/eval_jaxpr/dot_general | solution.py:51
  353.1 1.4 fusion.31
  354.5 0.0 copy-done.1
  354.5 2.3 fusion.30
  (54 shorter events, 0.8 us)
Async XLA Ops:
  6.5 75.3 %copy-start = (bf16[256,256]{1,0:T(8,128)(2,1)S(1)}, bf16[256,256]{1,0:T(8,128)(2,1)}, u32[]{:S(2)}) copy-start(bf16[256,256]{1,0:T(8,128)(2,1)} %param.11) | copy-start | bytes 393220
  6.5 62.5 %all-gather.2.cloned.1.call-start = ((), (), s32[]{:S(2)}) async-start(), calls=%async_computation | async-start | bytes 4718592 | tf_op jit(solution)/shard_map/all_gather | solution.py:40
  69.0 101.2 %collective-permute-start = (bf16[8192,256]{1,0:T(8,128)(2,1)}, bf16[8192,256]{1,0:T(8,128)(2,1)}, u32[]{:S(2)}, u32[]{:S(2)}) collective-permute-start(bf16[8192,256]{1,0:T(8,128)(2,1)} %all-gather.2.cloned.1.call-done), channel_id=1, source_target_pairs={{0,8},{8,16},{16,24},{24,32},{32,40},{40,48},{48,56},{56,64},{64,7... | collective-permute-start | bytes 12582920 | tf_op jit(solution)/shard_map/ppermute | solution.py:16
  71.0 100.2 %collective-permute-start.1 = (bf16[8192,256]{1,0:T(8,128)(2,1)}, bf16[8192,256]{1,0:T(8,128)(2,1)}, u32[]{:S(2)}, u32[]{:S(2)}) collective-permute-start(bf16[8192,256]{1,0:T(8,128)(2,1)} %all-gather.2.cloned.1.call-done), channel_id=1, source_target_pairs={{8,0},{16,8},{24,16},{32,24},{40,32},{48,40},{56,48},{64,56},{72,6... | collective-permute-start | bytes 12582920 | tf_op jit(solution)/shard_map/ppermute | solution.py:17
  186.5 168.0 %copy-start.1 = (bf16[256,256]{1,0:T(8,128)(2,1)S(1)}, bf16[256,256]{1,0:T(8,128)(2,1)}, u32[]{:S(2)}) copy-start(bf16[256,256]{1,0:T(8,128)(2,1)} %param.12) | copy-start | bytes 393220
  186.5 168.0 %copy-start.2 = (f32[256]{0:T(256)S(1)}, f32[256]{0:T(256)}, u32[]{:S(2)}) copy-start(f32[256]{0:T(256)} %param.13) | copy-start | bytes 3076
Sparse Core Ops, SparseCore 0:
  9.5 59.4 all-gather.1
where the time goes:
time: 365 us; the launch traced here: 364 us
  waiting for transfers between devices  149 us (41%)
  other arithmetic  78.9 us (22%)
  matrix products  59.5 us (16%)
  local copies, waits for them, and re-layouts  50.1 us (14%)
  between operations  13.5 us (4%)
  starting transfers between devices  12.1 us (3%)
    ppermute x1, waiting for transfers between devices, with_halo(): before = lax.ppermute(last, axis, up)  86 us
    all_gather x1, waiting for transfers between devices, shards(): grouped = lax.all_gather(features, 'rep', axis=0, tiled=True)  61.8 us
    reduce_sum x8, other arithmetic, one_row(): degree = jnp.sum(counts.astype(jnp.float32), axis=1)  60.9 us
    dot_general x8, matrix products, one_row(): jnp.dot(counts.astype(jnp.bfloat16), gathered, preferred_element_type=jnp...  54.8 us
    gather x8, local copies, waits for them, and re-layouts, one_row(): gathered = jnp.take(blocks, cols, axis=0).reshape(-1, width)  42.5 us
    concatenate x1, other arithmetic, with_halo(): value = jnp.concatenate([before, value, after], axis=dim)  15.4 us
    ppermute x1, starting transfers between devices, with_halo(): after = lax.ppermute(leading, axis, down)  10.2 us
  transfers between devices with their start and end apart: 3, of which 3 were waited for; matrix products, arithmetic and copies ran while one was open for 1% of the time, Pallas kernels for 0%

commit v1 on v0

v1 whole, which is shorter than its diff:
```python
import functools

import jax
import jax.numpy as jnp
from jax import lax
from jax.experimental import pallas as pl
from jax.experimental.pallas import tpu as pltpu
from jax.sharding import PartitionSpec as P

BS = 128
ROWS = 8
NNZB = 44
WIDTH = 256
CHUNK = 8
LIST = 48
PHASES = ((0, 1, 2, 3, 4, 8), (5, 6, 7, 9, 10, 11))


def unpack(words):
    column = jnp.right_shift(words, 2).astype(jnp.float32).astype(jnp.bfloat16)
    value = jnp.bitwise_and(words, 3).astype(jnp.float32).astype(jnp.bfloat16)
    place = lax.broadcasted_iota(jnp.int32, (BS, BS), 0).astype(jnp.float32).astype(jnp.bfloat16)
    counts = None
    for edge in range(4):
        at = jnp.broadcast_to(column[edge : edge + 1], (BS, BS))
        much = jnp.broadcast_to(value[edge : edge + 1], (BS, BS))
        term = jnp.where(at == place, much, jnp.bfloat16(0))
        counts = term if counts is None else counts + term
    return counts


def aggregate_kernel(pieces, resumed, count_ref, list_ref, words_ref, *refs):
    parts = refs[:pieces]
    refs = refs[pieces:]
    if resumed:
        before_ref, out_ref, window, sems = refs
    else:
        out_ref, window, sems = refs
    copies = [
        pltpu.make_async_copy(part, window.at[pl.ds(i * 8 * BS, 8 * BS)], sems.at[i]) for i, part in enumerate(parts)
    ]
    for copy in copies:
        copy.start()
    for copy in copies:
        copy.wait()

    def row(r, _):
        if resumed:
            out_ref[r] = before_ref[r]
        else:
            out_ref[r] = jnp.zeros((BS, WIDTH), jnp.float32)
        count = count_ref[r]

        def chunk(c, _):
            left = []
            right = []
            for u in range(CHUNK):
                entry = c * CHUNK + u
                code = list_ref[r, entry]
                words = words_ref[r, lax.shift_right_logical(code, 7)]
                words = jnp.where(entry < count, words, 0)
                left.append(unpack(words))
                block = jnp.bitwise_and(code, 127)
                right.append(window[pl.ds(pl.multiple_of(block * BS, BS), BS), :])
            left = jnp.concatenate(left, axis=0)
            right = jnp.concatenate(right, axis=0)
            out_ref[r] += lax.dot_general(left, right, (((0,), (0,)), ((), ())), preferred_element_type=jnp.float32)
            return 0

        lax.fori_loop(0, (count + CHUNK - 1) // CHUNK, chunk, 0)
        return 0

    lax.fori_loop(0, ROWS, row, 0)


def aggregate(count, entries, words, parts, before):
    smem = pl.BlockSpec(memory_space=pltpu.SMEM)
    vmem = pl.BlockSpec(memory_space=pltpu.VMEM)
    resumed = before is not None
    return pl.pallas_call(
        functools.partial(aggregate_kernel, len(parts), resumed),
        out_shape=jax.ShapeDtypeStruct((ROWS, BS, WIDTH), jnp.float32),
        in_specs=[smem, smem, vmem] + [pl.BlockSpec(memory_space=pl.ANY)] * len(parts) + [vmem] * resumed,
        out_specs=vmem,
        scratch_shapes=[
            pltpu.VMEM((len(parts) * 8 * BS, WIDTH), jnp.bfloat16),
            pltpu.SemaphoreType.DMA((len(parts),)),
        ],
        compiler_params=pltpu.CompilerParams(vmem_limit_bytes=40 * 2**20),
        cost_estimate=pl.CostEstimate(flops=4 * 2**28 * len(parts), bytes_accessed=2**22, transcendentals=0),
        name="aggregate",
    )(count, entries, words, *parts, *([before] if resumed else []))


def finish_kernel(own_ref, sent_ref, degree_ref, features_ref, self_ref, neigh_ref, bias_ref, out_ref):
    degree = jnp.maximum(degree_ref[...], 1.0).T
    for r in range(ROWS):
        at = pl.ds(r * BS, BS)
        mean = ((own_ref[r] + sent_ref[r]) / degree[:, r : r + 1]).astype(jnp.bfloat16)
        total = jnp.dot(features_ref[at, :], self_ref[...], preferred_element_type=jnp.float32)
        total = total + jnp.dot(mean, neigh_ref[...], preferred_element_type=jnp.float32) + bias_ref[...]
        out_ref[at, :] = jnp.maximum(total, 0.0).astype(jnp.bfloat16)


def finish(own, sent, degree, features, w_self, w_neigh, bias):
    vmem = pl.BlockSpec(memory_space=pltpu.VMEM)
    return pl.pallas_call(
        finish_kernel,
        out_shape=jax.ShapeDtypeStruct((ROWS * BS, WIDTH), jnp.bfloat16),
        in_specs=[vmem] * 7,
        out_specs=vmem,
        compiler_params=pltpu.CompilerParams(vmem_limit_bytes=16 * 2**20),
        cost_estimate=pl.CostEstimate(flops=2**28, bytes_accessed=2**22, transcendentals=0),
        name="finish",
    )(own, sent, degree, features, w_self, w_neigh, bias.reshape(1, -1))


def lists(cols):
    loop, group = lax.axis_size("blk"), lax.axis_size("rep")
    mine, rep = lax.axis_index("blk"), lax.axis_index("rep")
    side = (cols // (group * ROWS) - mine + loop) % loop
    side = jnp.where(side == loop - 1, 1, jnp.where(side == 1, 2, side))
    owner = cols // ROWS % group
    away = (owner // 2 - rep // 2 + group // 2) % (group // 2)
    piece = jnp.where(owner % 2 == rep % 2, side * (group // 2) + away, -1)
    out = []
    slot = jnp.arange(NNZB, dtype=jnp.int32)
    for phase in PHASES:
        place = jnp.full(cols.shape, -1, jnp.int32)
        for i, p in enumerate(phase):
            place = jnp.where(piece == p, i, place)
        held = place >= 0
        code = slot * 128 + place * 8 + cols % ROWS
        rank = jnp.sum(held[:, None, :] & (slot[None, None, :] < slot[None, :, None]), axis=2, dtype=jnp.int32)
        spot = jnp.arange(LIST, dtype=jnp.int32)
        hit = held[:, None, :] & (rank[:, None, :] == spot[None, :, None])
        entries = jnp.sum(jnp.where(hit, code[:, None, :], 0), axis=2, dtype=jnp.int32)
        out.append((jnp.sum(held, axis=1, dtype=jnp.int32), entries))
    return out


def shards(features, block_cols, adjacency, w_self, w_neigh, bias):
    devices, loop = lax.axis_size("rep"), lax.axis_size("blk")
    sibling = [(r, r ^ 1) for r in range(devices)]
    away = [[(r, (r - 2 * d) % devices) for r in range(devices)] for d in range(4)]
    up = [(i, (i + 1) % loop) for i in range(loop)]
    down = [(j, i) for i, j in up]

    noted = jnp.pad(block_cols[:, None, None, :], ((0, 0), (0, 0), (0, 3), (0, BS - NNZB)))
    words = jnp.concatenate([adjacency, noted], axis=1)
    theirs = lax.ppermute(words, "rep", sibling)
    own = [features] + [lax.ppermute(features, "rep", away[d]) for d in (1, 3, 2)]
    own = [own[0], own[1], own[3], own[2]]
    before = [lax.ppermute(part, "blk", up) for part in own]
    after = [lax.ppermute(part, "blk", down) for part in own]
    pieces = own + before + after

    mine_lists = lists(block_cols)
    their_lists = lists(theirs[:, NNZB, 0, :NNZB])
    degree = jnp.sum(jnp.bitwise_and(adjacency, 3), axis=(1, 2)).astype(jnp.float32)

    sums = []
    for w, entries in ((theirs, their_lists), (words, mine_lists)):
        total = None
        for phase, (count, listed) in zip(PHASES, entries):
            total = aggregate(count, listed, w, [pieces[p] for p in phase], total)
        sums.append(total)
    sent = lax.ppermute(sums[0], "rep", sibling)
    return finish(sums[1], sent, degree, features, w_self, w_neigh, bias)


def solution(mesh):
    in_specs = (
        P(("blk", "rep"), None),
        P(("blk", "rep"), None),
        P(("blk", "rep"), None, None, None),
        P(),
        P(),
        P(),
    )
    out_specs = P(("blk", "rep"), None)
    return jax.shard_map(shards, mesh=mesh, in_specs=in_specs, out_specs=out_specs, check_vma=False)
```

time: 365 us -> 146 us (0.40)
  waiting for transfers between devices: 149 us -> 52.7 us
  other arithmetic: 78.9 us -> 6.61 us
  matrix products: 59.5 us -> 0 us
  local copies, waits for them, and re-layouts: 50.1 us -> 2.13 us
  starting transfers between devices: 12.1 us -> 54 us
  Pallas kernels: 0 us -> 29.6 us
  between operations: 13.5 us -> 0.32 us
    all_gather x1 -> x0, waiting for transfers between devices: 61.8 us -> none  [shards(): grouped = lax.all_gather(features, 'rep', axis=0, tiled=True)]
    dot_general x10 -> x0, matrix products: 59.5 us -> none  [the longest x8 54.8 us: one_row(): jnp.dot(counts.astype(jnp.bfloat16), gathered, preferred_element_type=jnp...]
    reduce_sum x8 -> x6, other arithmetic: 60.9 us -> 5.31 us  [the longest x1 3.05 us: lists(): jnp.sum(held[:, None, :] & (slot[None, None, :] < slot[None, :, None]), a...]
    gather x8 -> x0, local copies, waits for them, and re-layouts: 42.5 us -> none  [one_row(): gathered = jnp.take(blocks, cols, axis=0).reshape(-1, width)]
    ppermute x2 -> x13, starting transfers between devices: 12.1 us -> 54 us  [the longest x4 20.5 us: shards(): after = [lax.ppermute(part, 'blk', down) for part in own]]
    ppermute x2 -> x13, waiting for transfers between devices: 86.8 us -> 52.7 us  [the longest x3 27.9 us: shards(): lax.ppermute(features, 'rep', away[d])]
    pallas_call x0 -> x5, Pallas kernels: none -> 29.6 us  [the longest x4 28.2 us: aggregate(): pl.pallas_call(functools.partial(aggregate_kernel, len(parts), resumed),...]
    concatenate x1, other arithmetic: 15.4 us -> 1.23 us  [shards(): words = jnp.concatenate([adjacency, noted], axis=1)]
  transfers between devices with their start and end apart: 3 -> 13, of which waited for: 3 -> 8; matrix products, arithmetic and copies ran while one was open for 1% -> 4% of each run, Pallas kernels for 0% -> 14%
where the time goes in v1:
time: 146 us; the launch traced here: 145 us
  starting transfers between devices  54 us (37%)
  waiting for transfers between devices  52.7 us (36%)
  Pallas kernels  29.6 us (20%)
  other arithmetic  6.61 us (5%)
  local copies, waits for them, and re-layouts  2.13 us (1%)
    pallas_call x4, Pallas kernels, aggregate(): pl.pallas_call(functools.partial(aggregate_kernel, len(parts), resumed),...  28.2 us
    ppermute x3, waiting for transfers between devices, shards(): lax.ppermute(features, 'rep', away[d])  27.9 us
    ppermute x4, waiting for transfers between devices, shards(): before = [lax.ppermute(part, 'blk', up) for part in own]  23.3 us
    ppermute x4, starting transfers between devices, shards(): after = [lax.ppermute(part, 'blk', down) for part in own]  20.5 us
    ppermute x3, starting transfers between devices, shards(): lax.ppermute(features, 'rep', away[d])  12.7 us
    ppermute x4, starting transfers between devices, shards(): before = [lax.ppermute(part, 'blk', up) for part in own]  9.51 us
    ppermute x1, starting transfers between devices, shards(): theirs = lax.ppermute(words, 'rep', sibling)  8.79 us
    reduce_sum x1, other arithmetic, lists(): jnp.sum(held[:, None, :] & (slot[None, None, :] < slot[None, :, None]), a...  3.05 us
  transfers between devices with their start and end apart: 13, of which 8 were waited for; matrix products, arithmetic and copies ran while one was open for 4% of the time, Pallas kernels for 14%

profile of v1, /device:TPU:1, one launch (start us, length us, event | category | flops | bytes accessed | tf_op | source)
XLA Modules:
  0.0 145.3 jit_solution(11908652370550000134)
XLA Ops:
  0.0 1.2 pad_add_fusion.words_ref
  1.2 8.8 %collective-permute-start.11 = (s32[8,45,4,128]{3,2,1,0:T(4,128)S(1)}, s32[8,45,4,128]{3,2,1,0:T(4,128)S(1)}, u32[]{:S(2)}, u32[]{:S(2)}) collective-permute-start(s32[8,45,4,128]{3,2,1,0:T(4,128)S(1)} %pad_add_fusion.words_ref), channel_id=1, source_target_pairs={{0,1},{1,0},{2,3},{3,2},{4,5},{5,4},{6,7},{7,6},{8,9},{9,8},{10,11... | collective-permute-start | bytes 2211848 | tf_op jit(solution)/shard_map/ppermute | solution.py:151
  10.0 8.5 %collective-permute-start.10 = (bf16[1024,256]{1,0:T(8,128)(2,1)S(1)}, bf16[1024,256]{1,0:T(8,128)(2,1)S(1)}, u32[]{:S(2)}, u32[]{:S(2)}) collective-permute-start(bf16[1024,256]{1,0:T(8,128)(2,1)S(1)} %copy-done), channel_id=1, source_target_pairs={{8,0},{16,8},{24,16},{32,24},{40,32},{48,40},{56,48},{64,56},{72,6... | collective-permute-start | bytes 1572872 | tf_op jit(solution)/shard_map/ppermute | solution.py:155
  18.6 1.9 %collective-permute-start.9 = (bf16[1024,256]{1,0:T(8,128)(2,1)S(1)}, bf16[1024,256]{1,0:T(8,128)(2,1)S(1)}, u32[]{:S(2)}, u32[]{:S(2)}) collective-permute-start(bf16[1024,256]{1,0:T(8,128)(2,1)S(1)} %copy-done), channel_id=1, source_target_pairs={{0,8},{8,16},{16,24},{24,32},{32,40},{40,48},{48,56},{56,64},{64,7... | collective-permute-start | bytes 1572872 | tf_op jit(solution)/shard_map/ppermute | solution.py:154
  20.5 4.2 %collective-permute-start.4 = (bf16[1024,256]{1,0:T(8,128)(2,1)S(1)}, bf16[1024,256]{1,0:T(8,128)(2,1)}, u32[]{:S(2)}, u32[]{:S(2)}) collective-permute-start(bf16[1024,256]{1,0:T(8,128)(2,1)S(1)} %copy-done), channel_id=1, source_target_pairs={{0,2},{1,3},{2,4},{3,5},{4,6},{5,7},{6,0},{7,1},{8,10},{9,11},{10,... | collective-permute-start | bytes 1572872 | tf_op jit(solution)/shard_map/ppermute | solution.py:152
  24.7 4.8 %collective-permute-start.2 = (bf16[1024,256]{1,0:T(8,128)(2,1)S(1)}, bf16[1024,256]{1,0:T(8,128)(2,1)}, u32[]{:S(2)}, u32[]{:S(2)}) collective-permute-start(bf16[1024,256]{1,0:T(8,128)(2,1)S(1)} %copy-done), channel_id=1, source_target_pairs={{0,4},{1,5},{2,6},{3,7},{4,0},{5,1},{6,2},{7,3},{8,12},{9,13},{10,... | collective-permute-start | bytes 1572872 | tf_op jit(solution)/shard_map/ppermute | solution.py:152
  29.5 1.3 and_reduce_fusion
  30.8 0.0 copy-start.4
  30.8 0.7 copy-done.4
  31.5 0.1 copy.10
  31.6 24.7 %collective-permute-done.4.refs_3_ = bf16[1024,256]{1,0:T(8,128)(2,1)} collective-permute-done((bf16[1024,256]{1,0:T(8,128)(2,1)S(1)}, bf16[1024,256]{1,0:T(8,128)(2,1)}, u32[]{:S(2)}, u32[]{:S(2)}) %collective-permute-start.4) | collective-permute-done | bytes 524320 | tf_op jit(solution)/shard_map/ppermute | solution.py:152
  56.3 3.8 %collective-permute-start = (bf16[1024,256]{1,0:T(8,128)(2,1)S(1)}, bf16[1024,256]{1,0:T(8,128)(2,1)}, u32[]{:S(2)}, u32[]{:S(2)}) collective-permute-start(bf16[1024,256]{1,0:T(8,128)(2,1)S(1)} %copy-done), channel_id=1, source_target_pairs={{0,6},{1,7},{2,0},{3,1},{4,2},{5,3},{6,4},{7,5},{8,14},{9,15},{10,... | collective-permute-start | bytes 1572872 | tf_op jit(solution)/shard_map/ppermute | solution.py:152
  60.0 1.9 %collective-permute-start.8 = (bf16[1024,256]{1,0:T(8,128)(2,1)}, bf16[1024,256]{1,0:T(8,128)(2,1)}, u32[]{:S(2)}, u32[]{:S(2)}) collective-permute-start(bf16[1024,256]{1,0:T(8,128)(2,1)} %collective-permute-done.4.refs_3_), channel_id=1, source_target_pairs={{8,0},{16,8},{24,16},{32,24},{40,32},{48,40},{56,48},{64,56},{72,6... | collective-permute-start | bytes 1572872 | tf_op jit(solution)/shard_map/ppermute | solution.py:155
  62.0 0.2 convert_reduce_fusion.6
  62.1 0.1 convert_reduce_fusion.5
  62.3 0.1 copy.11
  62.4 0.1 copy.13
  62.5 0.1 copy.9
  62.6 0.1 copy.7
  62.7 0.1 copy.12
  62.8 0.1 copy.8
  62.9 0.1 copy.14
  63.0 3.1 %convert_reduce_fusion = (s32[8,44]{0,1:T(8,128)S(1)}, s32[8,44]{0,1:T(8,128)S(1)}, s32[8,44]{0,1:T(8,128)S(1)}, s32[8,44]{0,1:T(8,128)S(1)}) fusion(pred[8,44]{1,0:T(8,128)(4,1)S(1)} %get-tuple-element.23, pred[44,44]{1,0:T(8,128)(4,1)S(1)} %iota_compare_fusion.4, pred[8,44]{1,0:T(8,128)(4,1)S(1)} %get-tuple-element.18, ...), kind=kLoop, calls=%fused_computation.4 | loop fusion | flops 184448 | bytes 8976 | tf_op jit(solution)/shard_map/reduce_sum | solution.py:134
  66.1 0.3 select_reduce_fusion.2
  66.4 0.3 select_reduce_fusion
  66.8 0.0 collective-permute-done.10.refs_5_
  66.8 3.4 %collective-permute-start.5 = (bf16[1024,256]{1,0:T(8,128)(2,1)}, bf16[1024,256]{1,0:T(8,128)(2,1)S(1)}, u32[]{:S(2)}, u32[]{:S(2)}) collective-permute-start(bf16[1024,256]{1,0:T(8,128)(2,1)} %collective-permute-done.4.refs_3_), channel_id=1, source_target_pairs={{0,8},{8,16},{16,24},{24,32},{32,40},{40,48},{48,56},{56,64},{64,7... | collective-permute-start | bytes 1572872 | tf_op jit(solution)/shard_map/ppermute | solution.py:154
  70.1 3.2 %collective-permute-done.2.refs_2_ = bf16[1024,256]{1,0:T(8,128)(2,1)} collective-permute-done((bf16[1024,256]{1,0:T(8,128)(2,1)S(1)}, bf16[1024,256]{1,0:T(8,128)(2,1)}, u32[]{:S(2)}, u32[]{:S(2)}) %collective-permute-start.2) | collective-permute-done | bytes 524320 | tf_op jit(solution)/shard_map/ppermute | solution.py:152
  73.3 2.9 %collective-permute-start.7 = (bf16[1024,256]{1,0:T(8,128)(2,1)}, bf16[1024,256]{1,0:T(8,128)(2,1)S(1)}, u32[]{:S(2)}, u32[]{:S(2)}) collective-permute-start(bf16[1024,256]{1,0:T(8,128)(2,1)} %collective-permute-done.2.refs_2_), channel_id=1, source_target_pairs={{8,0},{16,8},{24,16},{32,24},{40,32},{48,40},{56,48},{64,56},{72,6... | collective-permute-start | bytes 1572872 | tf_op jit(solution)/shard_map/ppermute | solution.py:155
  76.3 2.3 %collective-permute-start.3 = (bf16[1024,256]{1,0:T(8,128)(2,1)}, bf16[1024,256]{1,0:T(8,128)(2,1)S(1)}, u32[]{:S(2)}, u32[]{:S(2)}) collective-permute-start(bf16[1024,256]{1,0:T(8,128)(2,1)} %collective-permute-done.2.refs_2_), channel_id=1, source_target_pairs={{0,8},{8,16},{16,24},{24,32},{32,40},{40,48},{48,56},{56,64},{64,7... | collective-permute-start | bytes 1572872 | tf_op jit(solution)/shard_map/ppermute | solution.py:154
  78.7 7.2 %collective-permute-start.6 = (bf16[1024,256]{1,0:T(8,128)(2,1)}, bf16[1024,256]{1,0:T(8,128)(2,1)S(1)}, u32[]{:S(2)}, u32[]{:S(2)}) collective-permute-start(bf16[1024,256]{1,0:T(8,128)(2,1)} %collective-permute-done.refs_1_), channel_id=1, source_target_pairs={{8,0},{16,8},{24,16},{32,24},{40,32},{48,40},{56,48},{64,56},{72,6... | collective-permute-start | bytes 1572872 | tf_op jit(solution)/shard_map/ppermute | solution.py:155
  85.8 0.3 collective-permute-done.8.refs_5_
  86.2 1.9 %collective-permute-start.1 = (bf16[1024,256]{1,0:T(8,128)(2,1)}, bf16[1024,256]{1,0:T(8,128)(2,1)S(1)}, u32[]{:S(2)}, u32[]{:S(2)}) collective-permute-start(bf16[1024,256]{1,0:T(8,128)(2,1)} %collective-permute-done.refs_1_), channel_id=1, source_target_pairs={{0,8},{8,16},{16,24},{24,32},{32,40},{40,48},{48,56},{56,64},{64,7... | collective-permute-start | bytes 1572872 | tf_op jit(solution)/shard_map/ppermute | solution.py:154
  88.1 6.6 %aggregate.6.refs_6_ = f32[8,128,256]{2,1,0:T(8,128)S(1)} custom-call(s32[8]{0:T(128)S(1)} %get-tuple-element.22.count_ref, s32[8,48]{1,0:T(8,128)S(1)} %get-tuple-element.29.list_ref, s32[8,45,4,128]{3,2,1,0:T(4,128)S(1)} %collective-permute-done.11.words_ref, bf16[1024,256]{1,0:T(8,128)(2,1)S(1)} %copy-done, ...), custom_call_target="tpu_custom_call" | custom-call | flops 6442450944 | bytes 4194304 | tf_op jit(solution)/shard_map/aggregate/pallas_call | solution.py:80
  94.7 2.1 %collective-permute-done.5.refs_2_ = bf16[1024,256]{1,0:T(8,128)(2,1)S(1)} collective-permute-done((bf16[1024,256]{1,0:T(8,128)(2,1)}, bf16[1024,256]{1,0:T(8,128)(2,1)S(1)}, u32[]{:S(2)}, u32[]{:S(2)}) %collective-permute-start.5) | collective-permute-done | bytes 524320 | tf_op jit(solution)/shard_map/ppermute | solution.py:154
  96.8 0.6 collective-permute-done.7.refs_4_
  97.4 10.6 %collective-permute-done.3.refs_1_ = bf16[1024,256]{1,0:T(8,128)(2,1)S(1)} collective-permute-done((bf16[1024,256]{1,0:T(8,128)(2,1)}, bf16[1024,256]{1,0:T(8,128)(2,1)S(1)}, u32[]{:S(2)}, u32[]{:S(2)}) %collective-permute-start.3) | collective-permute-done | bytes 524320 | tf_op jit(solution)/shard_map/ppermute | solution.py:154
  108.0 0.6 collective-permute-done.6.refs_3_
  108.6 10.6 %collective-permute-done.1.refs_0_ = bf16[1024,256]{1,0:T(8,128)(2,1)S(1)} collective-permute-done((bf16[1024,256]{1,0:T(8,128)(2,1)}, bf16[1024,256]{1,0:T(8,128)(2,1)S(1)}, u32[]{:S(2)}, u32[]{:S(2)}) %collective-permute-start.1) | collective-permute-done | bytes 524320 | tf_op jit(solution)/shard_map/ppermute | solution.py:154
  119.2 7.1 %aggregate.7 = f32[8,128,256]{2,1,0:T(8,128)S(1)} custom-call(s32[8]{0:T(128)S(1)} %get-tuple-element.13.count_ref, s32[8,48]{1,0:T(8,128)S(1)} %get-tuple-element.30.list_ref, s32[8,45,4,128]{3,2,1,0:T(4,128)S(1)} %collective-permute-done.11.words_ref, bf16[1024,256]{1,0:T(8,128)(2,1)S(1)} %collective-permute-done.1.refs_0_, ...), custom_call_target="tpu_custom_call" | custom-call | flops 6442450944 | bytes 4194304 | tf_op jit(solution)/shard_map/aggregate/pallas_call | solution.py:80
  126.4 2.4 %collective-permute-start.12 = (f32[8,128,256]{2,1,0:T(8,128)S(1)}, f32[8,128,256]{2,1,0:T(8,128)S(1)}, u32[]{:S(2)}, u32[]{:S(2)}) collective-permute-start(f32[8,128,256]{2,1,0:T(8,128)S(1)} %aggregate.7), channel_id=1, source_target_pairs={{0,1},{1,0},{2,3},{3,2},{4,5},{5,4},{6,7},{7,6},{8,9},{9,8},{10,11... | collective-permute-start | bytes 3145736 | tf_op jit(solution)/shard_map/ppermute | solution.py:168
  128.8 7.3 %aggregate.4.refs_6_ = f32[8,128,256]{2,1,0:T(8,128)S(1)} custom-call(s32[8]{0:T(128)S(1)} %get-tuple-element.17.count_ref, s32[8,48]{1,0:T(8,128)S(1)} %get-tuple-element.31.list_ref, s32[8,45,4,128]{3,2,1,0:T(4,128)S(1)} %pad_add_fusion.words_ref, bf16[1024,256]{1,0:T(8,128)(2,1)S(1)} %copy-done, bf16[1024,256]{1,0:T(8,128)(2,1)} %collective-permute-done.refs_1_, ...), custom_call_target="tpu_custom_call" | custom-call | flops 6442450944 | bytes 4194304 | tf_op jit(solution)/shard_map/aggregate/pallas_call | solution.py:80
  136.1 0.0 copy-start.1
  136.1 0.0 copy-start.2
  136.1 7.1 %aggregate.5.own_ref = f32[8,128,256]{2,1,0:T(8,128)S(1)} custom-call(s32[8]{0:T(128)S(1)} %get-tuple-element.25.count_ref, s32[8,48]{1,0:T(8,128)S(1)} %get-tuple-element.32.list_ref, s32[8,45,4,128]{3,2,1,0:T(4,128)S(1)} %pad_add_fusion.words_ref, bf16[1024,256]{1,0:T(8,128)(2,1)S(1)} %collective-permute-done.1.refs_0_, ...), custom_call_target="tpu_custom_call" | custom-call | flops 6442450944 | bytes 4194304 | tf_op jit(solution)/shard_map/aggregate/pallas_call | solution.py:80
  143.2 0.0 copy-start.3
  143.3 0.6 copy-done.3
  143.9 1.4 finish.1
  (13 shorter events, 0.1 us)
Async XLA Ops:
  0.0 10.0 %copy-start = (bf16[1024,256]{1,0:T(8,128)(2,1)S(1)}, bf16[1024,256]{1,0:T(8,128)(2,1)}, u32[]{:S(2)}) copy-start(bf16[1024,256]{1,0:T(8,128)(2,1)} %features_ref.1) | copy-start | bytes 1572868
  1.2 58.8 %collective-permute-start.11 = (s32[8,45,4,128]{3,2,1,0:T(4,128)S(1)}, s32[8,45,4,128]{3,2,1,0:T(4,128)S(1)}, u32[]{:S(2)}, u32[]{:S(2)}) collective-permute-start(s32[8,45,4,128]{3,2,1,0:T(4,128)S(1)} %pad_add_fusion.words_ref), channel_id=1, source_target_pairs={{0,1},{1,0},{2,3},{3,2},{4,5},{5,4},{6,7},{7,6},{8,9},{9,8},{10,11... | collective-permute-start | bytes 2211848 | tf_op jit(solution)/shard_map/ppermute | solution.py:151
  10.0 56.7 %collective-permute-start.10 = (bf16[1024,256]{1,0:T(8,128)(2,1)S(1)}, bf16[1024,256]{1,0:T(8,128)(2,1)S(1)}, u32[]{:S(2)}, u32[]{:S(2)}) collective-permute-start(bf16[1024,256]{1,0:T(8,128)(2,1)S(1)} %copy-done), channel_id=1, source_target_pairs={{8,0},{16,8},{24,16},{32,24},{40,32},{48,40},{56,48},{64,56},{72,6... | collective-permute-start | bytes 1572872 | tf_op jit(solution)/shard_map/ppermute | solution.py:155
  18.6 57.7 %collective-permute-start.9 = (bf16[1024,256]{1,0:T(8,128)(2,1)S(1)}, bf16[1024,256]{1,0:T(8,128)(2,1)S(1)}, u32[]{:S(2)}, u32[]{:S(2)}) collective-permute-start(bf16[1024,256]{1,0:T(8,128)(2,1)S(1)} %copy-done), channel_id=1, source_target_pairs={{0,8},{8,16},{16,24},{24,32},{32,40},{40,48},{48,56},{56,64},{64,7... | collective-permute-start | bytes 1572872 | tf_op jit(solution)/shard_map/ppermute | solution.py:154
  20.5 35.8 %collective-permute-start.4 = (bf16[1024,256]{1,0:T(8,128)(2,1)S(1)}, bf16[1024,256]{1,0:T(8,128)(2,1)}, u32[]{:S(2)}, u32[]{:S(2)}) collective-permute-start(bf16[1024,256]{1,0:T(8,128)(2,1)S(1)} %copy-done), channel_id=1, source_target_pairs={{0,2},{1,3},{2,4},{3,5},{4,6},{5,7},{6,0},{7,1},{8,10},{9,11},{10,... | collective-permute-start | bytes 1572872 | tf_op jit(solution)/shard_map/ppermute | solution.py:152
  24.7 48.6 %collective-permute-start.2 = (bf16[1024,256]{1,0:T(8,128)(2,1)S(1)}, bf16[1024,256]{1,0:T(8,128)(2,1)}, u32[]{:S(2)}, u32[]{:S(2)}) collective-permute-start(bf16[1024,256]{1,0:T(8,128)(2,1)S(1)} %copy-done), channel_id=1, source_target_pairs={{0,4},{1,5},{2,6},{3,7},{4,0},{5,1},{6,2},{7,3},{8,12},{9,13},{10,... | collective-permute-start | bytes 1572872 | tf_op jit(solution)/shard_map/ppermute | solution.py:152
  30.8 0.7 copy-start.4
  56.3 22.4 %collective-permute-start = (bf16[1024,256]{1,0:T(8,128)(2,1)S(1)}, bf16[1024,256]{1,0:T(8,128)(2,1)}, u32[]{:S(2)}, u32[]{:S(2)}) collective-permute-start(bf16[1024,256]{1,0:T(8,128)(2,1)S(1)} %copy-done), channel_id=1, source_target_pairs={{0,6},{1,7},{2,0},{3,1},{4,2},{5,3},{6,4},{7,5},{8,14},{9,15},{10,... | collective-permute-start | bytes 1572872 | tf_op jit(solution)/shard_map/ppermute | solution.py:152
  60.0 26.1 %collective-permute-start.8 = (bf16[1024,256]{1,0:T(8,128)(2,1)}, bf16[1024,256]{1,0:T(8,128)(2,1)}, u32[]{:S(2)}, u32[]{:S(2)}) collective-permute-start(bf16[1024,256]{1,0:T(8,128)(2,1)} %collective-permute-done.4.refs_3_), channel_id=1, source_target_pairs={{8,0},{16,8},{24,16},{32,24},{40,32},{48,40},{56,48},{64,56},{72,6... | collective-permute-start | bytes 1572872 | tf_op jit(solution)/shard_map/ppermute | solution.py:155
  66.8 30.0 %collective-permute-start.5 = (bf16[1024,256]{1,0:T(8,128)(2,1)}, bf16[1024,256]{1,0:T(8,128)(2,1)S(1)}, u32[]{:S(2)}, u32[]{:S(2)}) collective-permute-start(bf16[1024,256]{1,0:T(8,128)(2,1)} %collective-permute-done.4.refs_3_), channel_id=1, source_target_pairs={{0,8},{8,16},{16,24},{24,32},{32,40},{40,48},{48,56},{56,64},{64,7... | collective-permute-start | bytes 1572872 | tf_op jit(solution)/shard_map/ppermute | solution.py:154
  73.3 24.0 %collective-permute-start.7 = (bf16[1024,256]{1,0:T(8,128)(2,1)}, bf16[1024,256]{1,0:T(8,128)(2,1)S(1)}, u32[]{:S(2)}, u32[]{:S(2)}) collective-permute-start(bf16[1024,256]{1,0:T(8,128)(2,1)} %collective-permute-done.2.refs_2_), channel_id=1, source_target_pairs={{8,0},{16,8},{24,16},{32,24},{40,32},{48,40},{56,48},{64,56},{72,6... | collective-permute-start | bytes 1572872 | tf_op jit(solution)/shard_map/ppermute | solution.py:155
  76.3 31.7 %collective-permute-start.3 = (bf16[1024,256]{1,0:T(8,128)(2,1)}, bf16[1024,256]{1,0:T(8,128)(2,1)S(1)}, u32[]{:S(2)}, u32[]{:S(2)}) collective-permute-start(bf16[1024,256]{1,0:T(8,128)(2,1)} %collective-permute-done.2.refs_2_), channel_id=1, source_target_pairs={{0,8},{8,16},{16,24},{24,32},{32,40},{40,48},{48,56},{56,64},{64,7... | collective-permute-start | bytes 1572872 | tf_op jit(solution)/shard_map/ppermute | solution.py:154
  78.7 30.0 %collective-permute-start.6 = (bf16[1024,256]{1,0:T(8,128)(2,1)}, bf16[1024,256]{1,0:T(8,128)(2,1)S(1)}, u32[]{:S(2)}, u32[]{:S(2)}) collective-permute-start(bf16[1024,256]{1,0:T(8,128)(2,1)} %collective-permute-done.refs_1_), channel_id=1, source_target_pairs={{8,0},{16,8},{24,16},{32,24},{40,32},{48,40},{56,48},{64,56},{72,6... | collective-permute-start | bytes 1572872 | tf_op jit(solution)/shard_map/ppermute | solution.py:155
  86.2 33.1 %collective-permute-start.1 = (bf16[1024,256]{1,0:T(8,128)(2,1)}, bf16[1024,256]{1,0:T(8,128)(2,1)S(1)}, u32[]{:S(2)}, u32[]{:S(2)}) collective-permute-start(bf16[1024,256]{1,0:T(8,128)(2,1)} %collective-permute-done.refs_1_), channel_id=1, source_target_pairs={{0,8},{8,16},{16,24},{24,32},{32,40},{40,48},{48,56},{56,64},{64,7... | collective-permute-start | bytes 1572872 | tf_op jit(solution)/shard_map/ppermute | solution.py:154
  126.4 16.9 %collective-permute-start.12 = (f32[8,128,256]{2,1,0:T(8,128)S(1)}, f32[8,128,256]{2,1,0:T(8,128)S(1)}, u32[]{:S(2)}, u32[]{:S(2)}) collective-permute-start(f32[8,128,256]{2,1,0:T(8,128)S(1)} %aggregate.7), channel_id=1, source_target_pairs={{0,1},{1,0},{2,3},{3,2},{4,5},{5,4},{6,7},{7,6},{8,9},{9,8},{10,11... | collective-permute-start | bytes 3145736 | tf_op jit(solution)/shard_map/ppermute | solution.py:168
  136.1 7.2 %copy-start.1 = (bf16[256,256]{1,0:T(8,128)(2,1)S(1)}, bf16[256,256]{1,0:T(8,128)(2,1)}, u32[]{:S(2)}) copy-start(bf16[256,256]{1,0:T(8,128)(2,1)} %self_ref.1) | copy-start | bytes 393220
  136.1 7.2 %copy-start.2 = (bf16[256,256]{1,0:T(8,128)(2,1)S(1)}, bf16[256,256]{1,0:T(8,128)(2,1)}, u32[]{:S(2)}) copy-start(bf16[256,256]{1,0:T(8,128)(2,1)} %neigh_ref.1) | copy-start | bytes 393220
  143.2 0.7 copy-start.3

commit v2 on v1

v2 whole, which is shorter than its diff:
```python
import functools

import jax
import jax.numpy as jnp
from jax import lax
from jax.experimental import pallas as pl
from jax.experimental.pallas import tpu as pltpu
from jax.sharding import PartitionSpec as P

BS = 128
ROWS = 8
NNZB = 44
WIDTH = 256
CODED = 4 * NNZB


def unpack(words):
    column = jnp.right_shift(words, 2).astype(jnp.float32).astype(jnp.bfloat16)
    value = jnp.bitwise_and(words, 3).astype(jnp.float32).astype(jnp.bfloat16)
    place = lax.broadcasted_iota(jnp.int32, (BS, BS), 0).astype(jnp.float32).astype(jnp.bfloat16)
    counts = None
    for edge in range(4):
        at = jnp.broadcast_to(column[edge : edge + 1], (BS, BS))
        much = jnp.broadcast_to(value[edge : edge + 1], (BS, BS))
        term = jnp.where(at == place, much, jnp.bfloat16(0))
        counts = term if counts is None else counts + term
    return counts


def total_of(before_ref, r, value):
    return value if before_ref is None else before_ref[r] + value


def aggregate_kernel(sources, kinds, width, together, pieces, resumed, narrow, list_ref, *refs):
    words = refs[:sources]
    parts = refs[sources : sources + pieces]
    refs = refs[sources + pieces :]
    befores = [None] * sources
    if resumed:
        befores, refs = refs[:sources], refs[sources:]
    outs, refs = refs[:sources], refs[sources:]
    totals = outs
    if narrow:
        totals, refs = [refs[0].at[i] for i in range(sources)], refs[1:]
    window, coded, sems = refs
    copies = []
    for i, ref in enumerate(parts):
        to = window.at[pl.ds(i * 8 * BS, 8 * BS)]
        copies.append(pltpu.make_async_copy(ref, to, sems.at[i]))
    for copy in copies:
        copy.start()
    for source in range(sources):
        for r in range(ROWS):
            coded[source, r] = words[source][r, :CODED, :].astype(jnp.int32)
    for copy in copies:
        copy.wait()

    for source in range(sources):
        out_ref = totals[source]
        kind = kinds[source]

        def chunk(r, c):
            count = list_ref[r, kind, BS - 1]
            left = []
            right = []
            for u in range(width):
                entry = c * width + u
                code = list_ref[r, kind, entry]
                at = pl.multiple_of(lax.shift_right_logical(code, 7) * 4, 4)
                some = jnp.where(entry < count, coded[source, r, pl.ds(at, 4), :], 0)
                left.append(unpack(some))
                block = jnp.bitwise_and(code, 127)
                right.append(window[pl.ds(pl.multiple_of(block * BS, BS), BS), :])
            left = jnp.concatenate(left, axis=0)
            right = jnp.concatenate(right, axis=0)
            return lax.dot_general(left, right, (((0,), (0,)), ((), ())), preferred_element_type=jnp.float32)

        def rows(i, _):
            for j in range(together):
                r = i * together + j
                out_ref[r] = total_of(befores[source], r, chunk(r, 0))
            for j in range(together):
                r = i * together + j

                def more(c, _):
                    out_ref[r] += chunk(r, c)
                    return 0

                lax.fori_loop(1, (list_ref[r, kind, BS - 1] + width - 1) // width, more, 0)
            return 0

        lax.fori_loop(0, ROWS // together, rows, 0)
        if narrow:
            lane = lax.broadcasted_iota(jnp.int32, (BS, BS), 1)
            scales = jnp.zeros((BS, BS), jnp.float32)
            for r in range(ROWS):
                value = out_ref[r]
                most = jnp.max(jnp.abs(value), axis=1, keepdims=True)
                power = jnp.ceil(jnp.log2(jnp.maximum(most, 2.0**-100))) - 14.0
                whole = jnp.round(value * jnp.exp2(-power))
                whole = jnp.clip(whole, -32767.0, 32767.0).astype(jnp.int32)
                outs[source][pl.ds(r * BS, BS), :] = whole.astype(jnp.int16)
                scales = jnp.where(lane == r, power, scales)
            tail = jnp.concatenate([scales.T[:16], jnp.zeros((16, BS), jnp.float32)], axis=1)
            outs[source][pl.ds(ROWS * BS, 16), :] = tail.astype(jnp.int32).astype(jnp.int16)


def aggregate(listed, words, kinds, parts, width, together, before=None, narrow=False):
    vmem = pl.BlockSpec(memory_space=pltpu.VMEM)
    whole = pl.BlockSpec(memory_space=pl.ANY)
    sources, pieces = len(words), len(parts)
    before = before or []
    shape = jax.ShapeDtypeStruct((ROWS, BS, WIDTH), jnp.float32)
    scratch = []
    if narrow:
        shape = jax.ShapeDtypeStruct((ROWS * BS + 16, WIDTH), jnp.int16)
        scratch = [pltpu.VMEM((sources, ROWS, BS, WIDTH), jnp.float32)]
    return pl.pallas_call(
        functools.partial(aggregate_kernel, sources, kinds, width, together, pieces, bool(before), narrow),
        out_shape=[shape] * sources,
        in_specs=[pl.BlockSpec(memory_space=pltpu.SMEM)] + [vmem] * sources + [whole] * pieces + [vmem] * len(before),
        out_specs=[vmem] * sources,
        scratch_shapes=scratch
        + [
            pltpu.VMEM((pieces * 8 * BS, WIDTH), jnp.bfloat16),
            pltpu.VMEM((sources, ROWS, CODED, BS), jnp.int32),
            pltpu.SemaphoreType.DMA((pieces,)),
        ],
        compiler_params=pltpu.CompilerParams(vmem_limit_bytes=40 * 2**20),
        cost_estimate=pl.CostEstimate(flops=5 * 2**30 * sources, bytes_accessed=2**23, transcendentals=0),
        name="aggregate",
    )(listed, *words, *parts, *before)


def finish_kernel(own_ref, up_ref, down_ref, degree_ref, features_ref, self_ref, neigh_ref, bias_ref, out_ref):
    degree = jnp.maximum(degree_ref[...], 1.0).T
    scales = []
    for ref in (up_ref, down_ref):
        tail = ref[pl.ds(ROWS * BS, 16), :BS].astype(jnp.int32).astype(jnp.float32)
        scales.append(jnp.exp2(tail[:ROWS]).T)
    for r in range(ROWS):
        at = pl.ds(r * BS, BS)
        total = own_ref[r]
        for ref, scale in zip((up_ref, down_ref), scales):
            total = total + ref[at, :].astype(jnp.int32).astype(jnp.float32) * scale[:, r : r + 1]
        mean = (total / degree[:, r : r + 1]).astype(jnp.bfloat16)
        total = jnp.dot(features_ref[at, :], self_ref[...], preferred_element_type=jnp.float32)
        total = total + jnp.dot(mean, neigh_ref[...], preferred_element_type=jnp.float32) + bias_ref[...]
        out_ref[at, :] = jnp.maximum(total, 0.0).astype(jnp.bfloat16)


def finish(own, up, down, degree, features, w_self, w_neigh, bias):
    vmem = pl.BlockSpec(memory_space=pltpu.VMEM)
    return pl.pallas_call(
        finish_kernel,
        out_shape=jax.ShapeDtypeStruct((ROWS * BS, WIDTH), jnp.bfloat16),
        in_specs=[vmem] * 8,
        out_specs=vmem,
        compiler_params=pltpu.CompilerParams(vmem_limit_bytes=16 * 2**20),
        cost_estimate=pl.CostEstimate(flops=2**28, bytes_accessed=2**22, transcendentals=0),
        name="finish",
    )(own, up, down, degree, features, w_self, w_neigh, bias.reshape(1, -1))


def lists(cols):
    loop, group = lax.axis_size("blk"), lax.axis_size("rep")
    mine, rep = lax.axis_index("blk"), lax.axis_index("rep")
    owner = cols // ROWS % group
    away = (owner // 2 - rep // 2 + group // 2) % (group // 2)
    other = owner % 2 != rep % 2
    side = (cols // (ROWS * group) - mine + loop) % loop
    late = away == 2
    slot = jnp.arange(NNZB, dtype=jnp.int32)
    base = slot * 128 + cols % ROWS
    order = jnp.where(late, 3, jnp.where(away == 3, 2, away))
    below, above, here = side == loop - 1, side == 1, side == 0
    kind = jnp.where(here, 4, jnp.where(above, 2, 0) + late.astype(jnp.int32))
    kind = jnp.where(below | above | here, kind, 5)
    place = jnp.where(here, order + jnp.where(other, 4, 0), order + jnp.where(other, 3, 0))
    place = jnp.where(late & ~here, jnp.where(other, 1, 0), place)
    code = base + place * 8
    ahead = slot[None, :] < slot[:, None]
    rank = jnp.sum(((kind[:, None, :] == kind[:, :, None]) & ahead).astype(jnp.int32), axis=2)
    spot = jnp.arange(5 * BS, dtype=jnp.int32)
    hit = (kind * BS + rank)[:, None, :] == spot[:, None]
    counted = (kind[:, None, :] == (spot // BS)[:, None]) & (spot % BS == BS - 1)[:, None]
    entries = jnp.sum(jnp.where(hit, code[:, None, :], 0) + counted.astype(jnp.int32), axis=2)
    return entries.reshape(ROWS, 5, BS)


def shards(features, block_cols, adjacency, w_self, w_neigh, bias):
    devices, loop = lax.axis_size("rep"), lax.axis_size("blk")
    sibling = [(r, r ^ 1) for r in range(devices)]
    away = [[(r, (r - 2 * d) % devices) for r in range(devices)] for d in range(4)]
    up = [(i, (i + 1) % loop) for i in range(loop)]
    down = [(j, i) for i, j in up]

    one = lax.ppermute(features, "rep", away[1])
    three = lax.ppermute(features, "rep", away[3])
    mine = lists(block_cols)
    words = jnp.concatenate([adjacency.reshape(ROWS, CODED, BS), jnp.pad(mine, ((0, 0), (0, 11), (0, 0)))], axis=1)
    words = words.astype(jnp.int16)
    upper = lax.ppermute(words, "blk", down)
    lower = lax.ppermute(words, "blk", up)
    listed = jnp.concatenate([upper[:, CODED : CODED + 2], lower[:, CODED + 2 : CODED + 4]], axis=1).astype(jnp.int32)
    listed = jnp.concatenate([listed, mine[:, 4:5]], axis=1)
    half = features.shape[0] // 2
    ahead = lax.ppermute(one[:half], "rep", away[1])
    behind = lax.ppermute(three[half:], "rep", away[3])
    early = [features, one, three]
    early = early + [lax.ppermute(part, "rep", sibling) for part in early]
    sums = aggregate(listed, [upper, lower], (0, 2), early, 12, 2)
    ahead, behind, *sums = lax.optimization_barrier((ahead, behind, *sums))
    two = jnp.concatenate([ahead, behind], axis=0)
    late = [two, lax.ppermute(two, "rep", sibling)]
    for_upper, for_lower = aggregate(listed, [upper, lower], (1, 3), late, 8, 4, sums, True)
    from_below = lax.ppermute(for_upper, "blk", up)
    from_above = lax.ppermute(for_lower, "blk", down)
    pieces = early[:3] + late[:1] + early[3:] + late[1:]
    coded, _ = lax.optimization_barrier((adjacency, for_upper))
    degree = jnp.sum(jnp.bitwise_and(coded, 3), axis=(1, 2)).astype(jnp.float32)
    (mine,) = aggregate(listed, [words], (4,), pieces, 16, 2)
    return finish(mine, from_below, from_above, degree, features, w_self, w_neigh, bias)


def solution(mesh):
    in_specs = (
        P(("blk", "rep"), None),
        P(("blk", "rep"), None),
        P(("blk", "rep"), None, None, None),
        P(),
        P(),
        P(),
    )
    out_specs = P(("blk", "rep"), None)
    return jax.shard_map(shards, mesh=mesh, in_specs=in_specs, out_specs=out_specs, check_vma=False)
```

time: 146 us -> 102 us (0.70)
  waiting for transfers between devices: 52.7 us -> 24.8 us
  Pallas kernels: 29.6 us -> 21.5 us
  other arithmetic: 6.61 us -> 2.77 us
  starting transfers between devices: 54 us -> 51.5 us
    ppermute x13 -> x12, waiting for transfers between devices: 52.7 us -> 24.8 us  [the longest x1 14.5 us: shards(): lower = lax.ppermute(words, 'blk', up)]
    pallas_call x4 -> x3, Pallas kernels: 28.2 us -> 19.8 us  [aggregate(): pl.pallas_call(functools.partial(aggregate_kernel, sources, kinds, width,...]
    reduce_sum x6 -> x3, other arithmetic: 5.31 us -> 1.32 us  [the longest x1 0.89 us: lists(): jnp.sum(((kind[:, None, :] == kind[:, :, None]) & ahead).astype(jnp.int32...]
    ppermute x13 -> x12, starting transfers between devices: 54 us -> 51.5 us  [the longest x1 12.3 us: shards(): upper = lax.ppermute(words, 'blk', down)]
  transfers between devices with their start and end apart: 13 -> 12, of which waited for: 8 -> 5; matrix products, arithmetic and copies ran while one was open for 4% -> 3% of each run, Pallas kernels for 14% -> 14%
where the time goes in v2:
time: 102 us
  starting transfers between devices  51.5 us (50%)
  waiting for transfers between devices  24.8 us (24%)
  Pallas kernels  21.5 us (21%)
  other arithmetic  2.77 us (3%)
    pallas_call x3, Pallas kernels, aggregate(): pl.pallas_call(functools.partial(aggregate_kernel, sources, kinds, width,...  19.8 us
    ppermute x1, waiting for transfers between devices, shards(): lower = lax.ppermute(words, 'blk', up)  14.5 us
    ppermute x1, starting transfers between devices, shards(): upper = lax.ppermute(words, 'blk', down)  12.3 us
    ppermute x3, starting transfers between devices, shards(): early = early + [lax.ppermute(part, 'rep', sibling) for part in early]  7.91 us
    ppermute x1, starting transfers between devices, shards(): from_above = lax.ppermute(for_lower, 'blk', down)  7.58 us
    ppermute x1, starting transfers between devices, shards(): three = lax.ppermute(features, 'rep', away[3])  5.04 us
    ppermute x1, waiting for transfers between devices, shards(): from_above = lax.ppermute(for_lower, 'blk', down)  4.75 us
    ppermute x1, starting transfers between devices, shards(): ahead = lax.ppermute(one[:half], 'rep', away[1])  3.92 us
  transfers between devices with their start and end apart: 12, of which 5 were waited for; matrix products, arithmetic and copies ran while one was open for 3% of the time, Pallas kernels for 14%

profile of v2, /device:TPU:1, one launch (start us, length us, event | category | flops | bytes accessed | tf_op | source)
XLA Modules:
  0.0 101.9 jit_solution(2660215066976396391)
XLA Ops:
  0.0 5.0 %collective-permute-start.3 = (bf16[1024,256]{1,0:T(8,128)(2,1)}, bf16[1024,256]{1,0:T(8,128)(2,1)S(1)}, u32[]{:S(2)}, u32[]{:S(2)}) collective-permute-start(bf16[1024,256]{1,0:T(8,128)(2,1)} %features_ref.1), channel_id=1, source_target_pairs={{0,2},{1,3},{2,4},{3,5},{4,6},{5,7},{6,0},{7,1},{8,10},{9,11},{10,... | collective-permute-start | bytes 1572872 | tf_op jit(solution)/shard_map/ppermute | solution.py:199
  5.0 3.6 %collective-permute-start.2 = (bf16[1024,256]{1,0:T(8,128)(2,1)}, bf16[1024,256]{1,0:T(8,128)(2,1)S(1)}, u32[]{:S(2)}, u32[]{:S(2)}) collective-permute-start(bf16[1024,256]{1,0:T(8,128)(2,1)} %features_ref.1), channel_id=1, source_target_pairs={{0,6},{1,7},{2,0},{3,1},{4,2},{5,3},{6,4},{7,5},{8,14},{9,15},{10,... | collective-permute-start | bytes 1572872 | tf_op jit(solution)/shard_map/ppermute | solution.py:198
  8.7 0.0 copy-start.5
  8.7 0.7 copy-done.5
  9.4 0.1 copy.16
  9.5 0.1 fusion.9
  9.6 0.1 copy.20
  9.7 0.9 convert_reduce_fusion
  10.6 0.3 add_reduce_fusion
  10.9 1.2 %convert.9 = s16[8,44,4,128]{3,2,1,0:T(4,128)(2,1)S(1)} convert(s32[8,44,4,128]{3,2,1,0:T(4,128)} %param.8) | non-fusion elementwise | flops 180224 | bytes 1081344 | tf_op jit(solution)/shard_map/convert.4
  12.1 0.0 copy-start
  12.2 3.3 %collective-permute-start.1 = (s16[8,192,128]{2,1,0:T(8,128)(2,1)S(1)}, s16[8,192,128]{2,1,0:T(8,128)(2,1)S(1)}, u32[]{:S(2)}, u32[]{:S(2)}) collective-permute-start(s16[8,192,128]{2,1,0:T(8,128)(2,1)S(1)} %pad_add_fusion.refs_0_), channel_id=1, source_target_pairs={{0,8},{8,16},{16,24},{24,32},{32,40},{40,48},{48,56},{56,64},{64,7... | collective-permute-start | bytes 1179656 | tf_op jit(solution)/shard_map/ppermute | solution.py:204
  15.5 12.3 %collective-permute-start = (s16[8,192,128]{2,1,0:T(8,128)(2,1)S(1)}, s16[8,192,128]{2,1,0:T(8,128)(2,1)S(1)}, u32[]{:S(2)}, u32[]{:S(2)}) collective-permute-start(s16[8,192,128]{2,1,0:T(8,128)(2,1)S(1)} %pad_add_fusion.refs_0_), channel_id=1, source_target_pairs={{8,0},{16,8},{24,16},{32,24},{40,32},{48,40},{56,48},{64,56},{72,6... | collective-permute-start | bytes 1179656 | tf_op jit(solution)/shard_map/ppermute | solution.py:203
  27.7 0.0 copy-done
  27.7 3.4 %collective-permute-start.6 = (bf16[1024,256]{1,0:T(8,128)(2,1)S(1)}, bf16[1024,256]{1,0:T(8,128)(2,1)S(1)}, u32[]{:S(2)}, u32[]{:S(2)}) collective-permute-start(bf16[1024,256]{1,0:T(8,128)(2,1)S(1)} %copy-done), channel_id=1, source_target_pairs={{0,1},{1,0},{2,3},{3,2},{4,5},{5,4},{6,7},{7,6},{8,9},{9,8},{10,11... | collective-permute-start | bytes 1572872 | tf_op jit(solution)/shard_map/ppermute | solution.py:211
  31.2 0.0 collective-permute-done.3.refs_4_.refs_3_
  31.2 1.9 %collective-permute-start.8 = (bf16[1024,256]{1,0:T(8,128)(2,1)S(1)}, bf16[1024,256]{1,0:T(8,128)(2,1)S(1)}, u32[]{:S(2)}, u32[]{:S(2)}) collective-permute-start(bf16[1024,256]{1,0:T(8,128)(2,1)S(1)} %collective-permute-done.3.refs_4_.refs_3_), channel_id=1, source_target_pairs={{0,1},{1,0},{2,3},{3,2},{4,5},{5,4},{6,7},{7,6},{8,9},{9,8},{10,11... | collective-permute-start | bytes 1572872 | tf_op jit(solution)/shard_map/ppermute | solution.py:211
  33.1 1.1 %collective-permute-done.2.refs_3_.refs_2_ = bf16[1024,256]{1,0:T(8,128)(2,1)S(1)} collective-permute-done((bf16[1024,256]{1,0:T(8,128)(2,1)}, bf16[1024,256]{1,0:T(8,128)(2,1)S(1)}, u32[]{:S(2)}, u32[]{:S(2)}) %collective-permute-start.2) | collective-permute-done | bytes 524320 | tf_op jit(solution)/shard_map/ppermute | solution.py:198
  34.2 2.6 %collective-permute-start.7 = (bf16[1024,256]{1,0:T(8,128)(2,1)S(1)}, bf16[1024,256]{1,0:T(8,128)(2,1)S(1)}, u32[]{:S(2)}, u32[]{:S(2)}) collective-permute-start(bf16[1024,256]{1,0:T(8,128)(2,1)S(1)} %collective-permute-done.2.refs_3_.refs_2_), channel_id=1, source_target_pairs={{0,1},{1,0},{2,3},{3,2},{4,5},{5,4},{6,7},{7,6},{8,9},{9,8},{10,11... | collective-permute-start | bytes 1572872 | tf_op jit(solution)/shard_map/ppermute | solution.py:211
  36.8 14.5 %collective-permute-done.1.refs_1_ = s16[8,192,128]{2,1,0:T(8,128)(2,1)S(1)} collective-permute-done((s16[8,192,128]{2,1,0:T(8,128)(2,1)S(1)}, s16[8,192,128]{2,1,0:T(8,128)(2,1)S(1)}, u32[]{:S(2)}, u32[]{:S(2)}) %collective-permute-start.1) | collective-permute-done | bytes 393248 | tf_op jit(solution)/shard_map/ppermute | solution.py:204
  51.3 0.0 collective-permute-done.refs_0_
  51.4 3.5 %collective-permute-start.5 = (bf16[512,256]{1,0:T(8,128)(2,1)S(1)}, bf16[512,256]{1,0:T(8,128)(2,1)S(1)}, u32[]{:S(2)}, u32[]{:S(2)}) collective-permute-start(bf16[512,256]{1,0:T(8,128)(2,1)S(1)} %slice.24), channel_id=1, source_target_pairs={{0,2},{1,3},{2,4},{3,5},{4,6},{5,7},{6,0},{7,1},{8,10},{9,11},{10,... | collective-permute-start | bytes 786440 | tf_op jit(solution)/shard_map/ppermute | solution.py:209
  54.9 3.9 %collective-permute-start.4 = (bf16[512,256]{1,0:T(8,128)(2,1)S(1)}, bf16[512,256]{1,0:T(8,128)(2,1)S(1)}, u32[]{:S(2)}, u32[]{:S(2)}) collective-permute-start(bf16[512,256]{1,0:T(8,128)(2,1)S(1)} %slice.23), channel_id=1, source_target_pairs={{0,6},{1,7},{2,0},{3,1},{4,2},{5,3},{6,4},{7,5},{8,14},{9,15},{10,... | collective-permute-start | bytes 786440 | tf_op jit(solution)/shard_map/ppermute | solution.py:208
  58.8 0.0 collective-permute-done.6.refs_5_
  58.8 0.0 collective-permute-done.8.refs_7_
  58.8 0.0 collective-permute-done.7.refs_6_
  58.9 8.5 %aggregate.3 = (f32[8,128,256]{2,1,0:T(8,128)S(1)}, f32[8,128,256]{2,1,0:T(8,128)S(1)}) custom-call(s32[8,5,128]{2,1,0:T(8,128)S(1)} %pad_add_fusion.1.list_ref, s16[8,192,128]{2,1,0:T(8,128)(2,1)S(1)} %collective-permute-done.refs_0_, s16[8,192,128]{2,1,0:T(8,128)(2,1)S(1)} %collective-permute-done.1.refs_1_, bf16[1024,256]{1,0:T(8,128)(2,1)S(1)} %copy-done, ...), custom_call_target="tpu_custom_call" | custom-call | flops 10737418240 | bytes 8388608 | tf_op jit(solution)/shard_map/aggregate/pallas_call | solution.py:118
  67.4 0.0 collective-permute-done.5
  67.4 2.9 %collective-permute-done.4 = bf16[512,256]{1,0:T(8,128)(2,1)S(1)} collective-permute-done((bf16[512,256]{1,0:T(8,128)(2,1)S(1)}, bf16[512,256]{1,0:T(8,128)(2,1)S(1)}, u32[]{:S(2)}, u32[]{:S(2)}) %collective-permute-start.4) | collective-permute-done | bytes 262176 | tf_op jit(solution)/shard_map/ppermute | solution.py:208
  70.4 0.0 copy-start.4
  70.4 2.5 %collective-permute-start.9 = (bf16[1024,256]{1,0:T(8,128)(2,1)S(1)}, bf16[1024,256]{1,0:T(8,128)(2,1)S(1)}, u32[]{:S(2)}, u32[]{:S(2)}) collective-permute-start(bf16[1024,256]{1,0:T(8,128)(2,1)S(1)} %constant_dynamic-update-slice_fusion.refs_4_.refs_2_), channel_id=1, source_target_pairs={{0,1},{1,0},{2,3},{3,2},{4,5},{5,4},{6,7},{7,6},{8,9},{9,8},{10,11... | collective-permute-start | bytes 1572872 | tf_op jit(solution)/shard_map/ppermute | solution.py:215
  72.9 1.5 %collective-permute-done.9.refs_8_.refs_3_ = bf16[1024,256]{1,0:T(8,128)(2,1)S(1)} collective-permute-done((bf16[1024,256]{1,0:T(8,128)(2,1)S(1)}, bf16[1024,256]{1,0:T(8,128)(2,1)S(1)}, u32[]{:S(2)}, u32[]{:S(2)}) %collective-permute-start.9) | collective-permute-done | bytes 524320 | tf_op jit(solution)/shard_map/ppermute | solution.py:215
  74.5 5.4 %aggregate.5 = (s16[1040,256]{1,0:T(8,128)(2,1)S(1)}, s16[1040,256]{1,0:T(8,128)(2,1)S(1)}) custom-call(s32[8,5,128]{2,1,0:T(8,128)S(1)} %pad_add_fusion.1.list_ref, s16[8,192,128]{2,1,0:T(8,128)(2,1)S(1)} %collective-permute-done.refs_0_, s16[8,192,128]{2,1,0:T(8,128)(2,1)S(1)} %collective-permute-done.1.refs_1_, ...), custom_call_target="tpu_custom_call" | custom-call | flops 10737418240 | bytes 8388608 | tf_op jit(solution)/shard_map/aggregate/pallas_call | solution.py:118
  79.9 1.9 %collective-permute-start.10 = (s16[1040,256]{1,0:T(8,128)(2,1)S(1)}, s16[1040,256]{1,0:T(8,128)(2,1)S(1)}, u32[]{:S(2)}, u32[]{:S(2)}) collective-permute-start(s16[1040,256]{1,0:T(8,128)(2,1)S(1)} %get-tuple-element.20), channel_id=1, source_target_pairs={{0,8},{8,16},{16,24},{24,32},{32,40},{40,48},{48,56},{56,64},{64,7... | collective-permute-start | bytes 1597448 | tf_op jit(solution)/shard_map/ppermute | solution.py:217
  81.8 7.6 %collective-permute-start.11 = (s16[1040,256]{1,0:T(8,128)(2,1)S(1)}, s16[1040,256]{1,0:T(8,128)(2,1)S(1)}, u32[]{:S(2)}, u32[]{:S(2)}) collective-permute-start(s16[1040,256]{1,0:T(8,128)(2,1)S(1)} %get-tuple-element.21), channel_id=1, source_target_pairs={{8,0},{16,8},{24,16},{32,24},{40,32},{48,40},{56,48},{64,56},{72,6... | collective-permute-start | bytes 1597448 | tf_op jit(solution)/shard_map/ppermute | solution.py:218
  89.4 0.0 copy-done.4
  89.4 0.2 and_reduce_fusion
  89.6 0.0 copy-start.1
  89.6 0.0 copy-start.2
  89.6 5.8 %aggregate.4.own_ref = f32[8,128,256]{2,1,0:T(8,128)S(1)} custom-call(s32[8,5,128]{2,1,0:T(8,128)S(1)} %pad_add_fusion.1.list_ref, s16[8,192,128]{2,1,0:T(8,128)(2,1)S(1)} %pad_add_fusion.refs_0_, bf16[1024,256]{1,0:T(8,128)(2,1)S(1)} %copy-done, bf16[1024,256]{1,0:T(8,128)(2,1)S(1)} %collective-permute-done.2.refs_3_.refs_2_, ...), custom_call_target="tpu_custom_call" | custom-call | flops 5368709120 | bytes 8388608 | tf_op jit(solution)/shard_map/aggregate/pallas_call | solution.py:118
  95.4 0.0 copy-start.3
  95.4 4.8 %collective-permute-done.11.down_ref = s16[1040,256]{1,0:T(8,128)(2,1)S(1)} collective-permute-done((s16[1040,256]{1,0:T(8,128)(2,1)S(1)}, s16[1040,256]{1,0:T(8,128)(2,1)S(1)}, u32[]{:S(2)}, u32[]{:S(2)}) %collective-permute-start.11) | collective-permute-done | bytes 532512 | tf_op jit(solution)/shard_map/ppermute | solution.py:218
  100.2 0.0 collective-permute-done.10.up_ref
  100.2 0.0 copy-done.1
  100.2 0.0 copy-done.2
  100.2 0.0 copy-done.3
  100.2 1.7 %finish.1 = bf16[1024,256]{1,0:T(8,128)(2,1)} custom-call(f32[8,128,256]{2,1,0:T(8,128)S(1)} %aggregate.4.own_ref, s16[1040,256]{1,0:T(8,128)(2,1)S(1)} %collective-permute-done.10.up_ref, s16[1040,256]{1,0:T(8,128)(2,1)S(1)} %collective-permute-done.11.down_ref, f32[8,128]{1,0:T(8,128)S(1)} %convert_element_type.20.degree_ref, ...), custom_call_target="tpu_custom_call" | custom-call | flops 268435456 | bytes 4194304 | tf_op jit(solution)/shard_map/finish/pallas_call | solution.py:154
  (18 shorter events, 0.2 us)
Async XLA Ops:
  0.0 31.2 %collective-permute-start.3 = (bf16[1024,256]{1,0:T(8,128)(2,1)}, bf16[1024,256]{1,0:T(8,128)(2,1)S(1)}, u32[]{:S(2)}, u32[]{:S(2)}) collective-permute-start(bf16[1024,256]{1,0:T(8,128)(2,1)} %features_ref.1), channel_id=1, source_target_pairs={{0,2},{1,3},{2,4},{3,5},{4,6},{5,7},{6,0},{7,1},{8,10},{9,11},{10,... | collective-permute-start | bytes 1572872 | tf_op jit(solution)/shard_map/ppermute | solution.py:199
  5.0 29.2 %collective-permute-start.2 = (bf16[1024,256]{1,0:T(8,128)(2,1)}, bf16[1024,256]{1,0:T(8,128)(2,1)S(1)}, u32[]{:S(2)}, u32[]{:S(2)}) collective-permute-start(bf16[1024,256]{1,0:T(8,128)(2,1)} %features_ref.1), channel_id=1, source_target_pairs={{0,6},{1,7},{2,0},{3,1},{4,2},{5,3},{6,4},{7,5},{8,14},{9,15},{10,... | collective-permute-start | bytes 1572872 | tf_op jit(solution)/shard_map/ppermute | solution.py:198
  8.7 0.7 copy-start.5
  12.1 15.6 %copy-start = (bf16[1024,256]{1,0:T(8,128)(2,1)S(1)}, bf16[1024,256]{1,0:T(8,128)(2,1)}, u32[]{:S(2)}) copy-start(bf16[1024,256]{1,0:T(8,128)(2,1)} %features_ref.1) | copy-start | bytes 1572868
  12.2 39.1 %collective-permute-start.1 = (s16[8,192,128]{2,1,0:T(8,128)(2,1)S(1)}, s16[8,192,128]{2,1,0:T(8,128)(2,1)S(1)}, u32[]{:S(2)}, u32[]{:S(2)}) collective-permute-start(s16[8,192,128]{2,1,0:T(8,128)(2,1)S(1)} %pad_add_fusion.refs_0_), channel_id=1, source_target_pairs={{0,8},{8,16},{16,24},{24,32},{32,40},{40,48},{48,56},{56,64},{64,7... | collective-permute-start | bytes 1179656 | tf_op jit(solution)/shard_map/ppermute | solution.py:204
  15.5 35.8 %collective-permute-start = (s16[8,192,128]{2,1,0:T(8,128)(2,1)S(1)}, s16[8,192,128]{2,1,0:T(8,128)(2,1)S(1)}, u32[]{:S(2)}, u32[]{:S(2)}) collective-permute-start(s16[8,192,128]{2,1,0:T(8,128)(2,1)S(1)} %pad_add_fusion.refs_0_), channel_id=1, source_target_pairs={{8,0},{16,8},{24,16},{32,24},{40,32},{48,40},{56,48},{64,56},{72,6... | collective-permute-start | bytes 1179656 | tf_op jit(solution)/shard_map/ppermute | solution.py:203
  27.7 31.1 %collective-permute-start.6 = (bf16[1024,256]{1,0:T(8,128)(2,1)S(1)}, bf16[1024,256]{1,0:T(8,128)(2,1)S(1)}, u32[]{:S(2)}, u32[]{:S(2)}) collective-permute-start(bf16[1024,256]{1,0:T(8,128)(2,1)S(1)} %copy-done), channel_id=1, source_target_pairs={{0,1},{1,0},{2,3},{3,2},{4,5},{5,4},{6,7},{7,6},{8,9},{9,8},{10,11... | collective-permute-start | bytes 1572872 | tf_op jit(solution)/shard_map/ppermute | solution.py:211
  31.2 27.7 %collective-permute-start.8 = (bf16[1024,256]{1,0:T(8,128)(2,1)S(1)}, bf16[1024,256]{1,0:T(8,128)(2,1)S(1)}, u32[]{:S(2)}, u32[]{:S(2)}) collective-permute-start(bf16[1024,256]{1,0:T(8,128)(2,1)S(1)} %collective-permute-done.3.refs_4_.refs_3_), channel_id=1, source_target_pairs={{0,1},{1,0},{2,3},{3,2},{4,5},{5,4},{6,7},{7,6},{8,9},{9,8},{10,11... | collective-permute-start | bytes 1572872 | tf_op jit(solution)/shard_map/ppermute | solution.py:211
  34.2 24.6 %collective-permute-start.7 = (bf16[1024,256]{1,0:T(8,128)(2,1)S(1)}, bf16[1024,256]{1,0:T(8,128)(2,1)S(1)}, u32[]{:S(2)}, u32[]{:S(2)}) collective-permute-start(bf16[1024,256]{1,0:T(8,128)(2,1)S(1)} %collective-permute-done.2.refs_3_.refs_2_), channel_id=1, source_target_pairs={{0,1},{1,0},{2,3},{3,2},{4,5},{5,4},{6,7},{7,6},{8,9},{9,8},{10,11... | collective-permute-start | bytes 1572872 | tf_op jit(solution)/shard_map/ppermute | solution.py:211
  51.4 16.0 %collective-permute-start.5 = (bf16[512,256]{1,0:T(8,128)(2,1)S(1)}, bf16[512,256]{1,0:T(8,128)(2,1)S(1)}, u32[]{:S(2)}, u32[]{:S(2)}) collective-permute-start(bf16[512,256]{1,0:T(8,128)(2,1)S(1)} %slice.24), channel_id=1, source_target_pairs={{0,2},{1,3},{2,4},{3,5},{4,6},{5,7},{6,0},{7,1},{8,10},{9,11},{10,... | collective-permute-start | bytes 786440 | tf_op jit(solution)/shard_map/ppermute | solution.py:209
  54.9 15.4 %collective-permute-start.4 = (bf16[512,256]{1,0:T(8,128)(2,1)S(1)}, bf16[512,256]{1,0:T(8,128)(2,1)S(1)}, u32[]{:S(2)}, u32[]{:S(2)}) collective-permute-start(bf16[512,256]{1,0:T(8,128)(2,1)S(1)} %slice.23), channel_id=1, source_target_pairs={{0,6},{1,7},{2,0},{3,1},{4,2},{5,3},{6,4},{7,5},{8,14},{9,15},{10,... | collective-permute-start | bytes 786440 | tf_op jit(solution)/shard_map/ppermute | solution.py:208
  70.4 19.0 %copy-start.4 = (s32[8,44,4,128]{3,2,1,0:T(4,128)S(1)}, s32[8,44,4,128]{3,2,1,0:T(4,128)}, u32[]{:S(2)}) copy-start(s32[8,44,4,128]{3,2,1,0:T(4,128)} %param.8) | copy-start | bytes 2162692
  70.4 4.1 %collective-permute-start.9 = (bf16[1024,256]{1,0:T(8,128)(2,1)S(1)}, bf16[1024,256]{1,0:T(8,128)(2,1)S(1)}, u32[]{:S(2)}, u32[]{:S(2)}) collective-permute-start(bf16[1024,256]{1,0:T(8,128)(2,1)S(1)} %constant_dynamic-update-slice_fusion.refs_4_.refs_2_), channel_id=1, source_target_pairs={{0,1},{1,0},{2,3},{3,2},{4,5},{5,4},{6,7},{7,6},{8,9},{9,8},{10,11... | collective-permute-start | bytes 1572872 | tf_op jit(solution)/shard_map/ppermute | solution.py:215
  79.9 20.3 %collective-permute-start.10 = (s16[1040,256]{1,0:T(8,128)(2,1)S(1)}, s16[1040,256]{1,0:T(8,128)(2,1)S(1)}, u32[]{:S(2)}, u32[]{:S(2)}) collective-permute-start(s16[1040,256]{1,0:T(8,128)(2,1)S(1)} %get-tuple-element.20), channel_id=1, source_target_pairs={{0,8},{8,16},{16,24},{24,32},{32,40},{40,48},{48,56},{56,64},{64,7... | collective-permute-start | bytes 1597448 | tf_op jit(solution)/shard_map/ppermute | solution.py:217
  81.8 18.4 %collective-permute-start.11 = (s16[1040,256]{1,0:T(8,128)(2,1)S(1)}, s16[1040,256]{1,0:T(8,128)(2,1)S(1)}, u32[]{:S(2)}, u32[]{:S(2)}) collective-permute-start(s16[1040,256]{1,0:T(8,128)(2,1)S(1)} %get-tuple-element.21), channel_id=1, source_target_pairs={{8,0},{16,8},{24,16},{32,24},{40,32},{48,40},{56,48},{64,56},{72,6... | collective-permute-start | bytes 1597448 | tf_op jit(solution)/shard_map/ppermute | solution.py:218
  89.6 10.6 %copy-start.1 = (bf16[256,256]{1,0:T(8,128)(2,1)S(1)}, bf16[256,256]{1,0:T(8,128)(2,1)}, u32[]{:S(2)}) copy-start(bf16[256,256]{1,0:T(8,128)(2,1)} %self_ref.1) | copy-start | bytes 393220
  89.6 10.6 %copy-start.2 = (bf16[256,256]{1,0:T(8,128)(2,1)S(1)}, bf16[256,256]{1,0:T(8,128)(2,1)}, u32[]{:S(2)}) copy-start(bf16[256,256]{1,0:T(8,128)(2,1)} %neigh_ref.1) | copy-start | bytes 393220
  95.4 4.8 %copy-start.3 = (f32[256]{0:T(256)S(1)}, f32[256]{0:T(256)}, u32[]{:S(2)}) copy-start(f32[256]{0:T(256)} %param.11) | copy-start | bytes 3076

commit v3 on v2

--- a/solution.py
+++ b/solution.py
@@ -31,7 +31,7 @@
     return value if before_ref is None else before_ref[r] + value
 
 
-def aggregate_kernel(sources, kinds, width, together, pieces, resumed, narrow, list_ref, *refs):
+def aggregate_kernel(sources, kinds, width, together, pieces, resumed, narrow, *refs):
     words = refs[:sources]
     parts = refs[sources : sources + pieces]
     refs = refs[sources + pieces :]
@@ -42,16 +42,23 @@
     totals = outs
     if narrow:
         totals, refs = [refs[0].at[i] for i in range(sources)], refs[1:]
-    window, coded, sems = refs
+    window, coded, noted, lists_ref, sems = refs
     copies = []
+    at = 0
     for i, ref in enumerate(parts):
-        to = window.at[pl.ds(i * 8 * BS, 8 * BS)]
-        copies.append(pltpu.make_async_copy(ref, to, sems.at[i]))
+        copies.append(pltpu.make_async_copy(ref, window.at[pl.ds(at, ref.shape[0])], sems.at[i]))
+        at += ref.shape[0]
     for copy in copies:
         copy.start()
     for source in range(sources):
         for r in range(ROWS):
+            noted[source, r] = words[source][r, CODED:, :].astype(jnp.int32)
+    scalars = pltpu.make_async_copy(noted.at[:, :, pl.ds(0, 8)], lists_ref, sems.at[pieces])
+    scalars.start()
+    for source in range(sources):
+        for r in range(ROWS):
             coded[source, r] = words[source][r, :CODED, :].astype(jnp.int32)
+    scalars.wait()
     for copy in copies:
         copy.wait()
 
@@ -60,12 +67,12 @@
         kind = kinds[source]
 
         def chunk(r, c):
-            count = list_ref[r, kind, BS - 1]
+            count = lists_ref[source, r, kind, BS - 1]
             left = []
             right = []
             for u in range(width):
                 entry = c * width + u
-                code = list_ref[r, kind, entry]
+                code = lists_ref[source, r, kind, entry]
                 at = pl.multiple_of(lax.shift_right_logical(code, 7) * 4, 4)
                 some = jnp.where(entry < count, coded[source, r, pl.ds(at, 4), :], 0)
                 left.append(unpack(some))
@@ -86,7 +93,7 @@
                     out_ref[r] += chunk(r, c)
                     return 0
 
-                lax.fori_loop(1, (list_ref[r, kind, BS - 1] + width - 1) // width, more, 0)
+                lax.fori_loop(1, (lists_ref[source, r, kind, BS - 1] + width - 1) // width, more, 0)
             return 0
 
         lax.fori_loop(0, ROWS // together, rows, 0)
@@ -105,7 +112,7 @@
             outs[source][pl.ds(ROWS * BS, 16), :] = tail.astype(jnp.int32).astype(jnp.int16)
 
 
-def aggregate(listed, words, kinds, parts, width, together, before=None, narrow=False):
+def aggregate(words, kinds, parts, width, together, before=None, narrow=False):
     vmem = pl.BlockSpec(memory_space=pltpu.VMEM)
     whole = pl.BlockSpec(memory_space=pl.ANY)
     sources, pieces = len(words), len(parts)
@@ -118,18 +125,20 @@
     return pl.pallas_call(
         functools.partial(aggregate_kernel, sources, kinds, width, together, pieces, bool(before), narrow),
         out_shape=[shape] * sources,
-        in_specs=[pl.BlockSpec(memory_space=pltpu.SMEM)] + [vmem] * sources + [whole] * pieces + [vmem] * len(before),
+        in_specs=[vmem] * sources + [whole] * pieces + [vmem] * len(before),
         out_specs=[vmem] * sources,
         scratch_shapes=scratch
         + [
-            pltpu.VMEM((pieces * 8 * BS, WIDTH), jnp.bfloat16),
+            pltpu.VMEM((sum(part.shape[0] for part in parts), WIDTH), jnp.bfloat16),
             pltpu.VMEM((sources, ROWS, CODED, BS), jnp.int32),
-            pltpu.SemaphoreType.DMA((pieces,)),
+            pltpu.VMEM((sources, ROWS, 16, BS), jnp.int32),
+            pltpu.SMEM((sources, ROWS, 8, BS), jnp.int32),
+            pltpu.SemaphoreType.DMA((pieces + 1,)),
         ],
         compiler_params=pltpu.CompilerParams(vmem_limit_bytes=40 * 2**20),
-        cost_estimate=pl.CostEstimate(flops=5 * 2**30 * sources, bytes_accessed=2**23, transcendentals=0),
+        cost_estimate=pl.CostEstimate(flops=0, bytes_accessed=0, transcendentals=0),
         name="aggregate",
-    )(listed, *words, *parts, *before)
+    )(*words, *parts, *before)
 
 
 def finish_kernel(own_ref, up_ref, down_ref, degree_ref, features_ref, self_ref, neigh_ref, bias_ref, out_ref):
@@ -169,15 +178,15 @@
     away = (owner // 2 - rep // 2 + group // 2) % (group // 2)
     other = owner % 2 != rep % 2
     side = (cols // (ROWS * group) - mine + loop) % loop
-    late = away == 2
     slot = jnp.arange(NNZB, dtype=jnp.int32)
     base = slot * 128 + cols % ROWS
-    order = jnp.where(late, 3, jnp.where(away == 3, 2, away))
+    late = (away == 2) | (other & (away != 0))
+    place = jnp.where(away == 0, 0, jnp.where(away == 1, 2, 3)) + jnp.where(other, 1, 0)
+    place = jnp.where(late, jnp.where(away == 2, 4, jnp.where(away == 1, 5, 6)) + jnp.where(other, 1, 0), place)
     below, above, here = side == loop - 1, side == 1, side == 0
     kind = jnp.where(here, 4, jnp.where(above, 2, 0) + late.astype(jnp.int32))
     kind = jnp.where(below | above | here, kind, 5)
-    place = jnp.where(here, order + jnp.where(other, 4, 0), order + jnp.where(other, 3, 0))
-    place = jnp.where(late & ~here, jnp.where(other, 1, 0), place)
+    place = jnp.where(late & ~here, place - 4, place)
     code = base + place * 8
     ahead = slot[None, :] < slot[:, None]
     rank = jnp.sum(((kind[:, None, :] == kind[:, :, None]) & ahead).astype(jnp.int32), axis=2)
@@ -202,24 +211,23 @@
     words = words.astype(jnp.int16)
     upper = lax.ppermute(words, "blk", down)
     lower = lax.ppermute(words, "blk", up)
-    listed = jnp.concatenate([upper[:, CODED : CODED + 2], lower[:, CODED + 2 : CODED + 4]], axis=1).astype(jnp.int32)
-    listed = jnp.concatenate([listed, mine[:, 4:5]], axis=1)
     half = features.shape[0] // 2
     ahead = lax.ppermute(one[:half], "rep", away[1])
     behind = lax.ppermute(three[half:], "rep", away[3])
-    early = [features, one, three]
-    early = early + [lax.ppermute(part, "rep", sibling) for part in early]
-    sums = aggregate(listed, [upper, lower], (0, 2), early, 12, 2)
+    both = jnp.concatenate([one, three], axis=0)
+    sib_own = lax.ppermute(features, "rep", sibling)
+    early = [features, sib_own, both]
+    sums = aggregate([upper, lower], (0, 2), early, 10, 2)
     ahead, behind, *sums = lax.optimization_barrier((ahead, behind, *sums))
     two = jnp.concatenate([ahead, behind], axis=0)
-    late = [two, lax.ppermute(two, "rep", sibling)]
-    for_upper, for_lower = aggregate(listed, [upper, lower], (1, 3), late, 8, 4, sums, True)
+    late = [two, lax.ppermute(two, "rep", sibling), lax.ppermute(both, "rep", sibling)]
+    for_upper, for_lower = aggregate([upper, lower], (1, 3), late, 10, 2, sums, True)
     from_below = lax.ppermute(for_upper, "blk", up)
     from_above = lax.ppermute(for_lower, "blk", down)
-    pieces = early[:3] + late[:1] + early[3:] + late[1:]
+    pieces = early + late
     coded, _ = lax.optimization_barrier((adjacency, for_upper))
     degree = jnp.sum(jnp.bitwise_and(coded, 3), axis=(1, 2)).astype(jnp.float32)
-    (mine,) = aggregate(listed, [words], (4,), pieces, 16, 2)
+    (mine,) = aggregate([words], (4,), pieces, 16, 2)
     return finish(mine, from_below, from_above, degree, features, w_self, w_neigh, bias)
 
 

time: 102 us -> 96.5 us (0.946)
  waiting for transfers between devices: 24.8 us -> 13.2 us
  starting transfers between devices: 51.5 us -> 55.6 us
  Pallas kernels: 21.5 us -> 23.1 us
    ppermute x1, waiting for transfers between devices: 14.5 us -> 4.84 us  [shards(): lower = lax.ppermute(words, 'blk', up)]
    ppermute x1, waiting for transfers between devices: 0.01 us -> 4.4 us  [shards(): from_below = lax.ppermute(for_upper, 'blk', up)]
    ppermute x1, waiting for transfers between devices: 4.75 us -> 0.87 us  [shards(): from_above = lax.ppermute(for_lower, 'blk', down)]
    ppermute x1, starting transfers between devices: 5.04 us -> 1.92 us  [shards(): three = lax.ppermute(features, 'rep', away[3])]
    ppermute x1, starting transfers between devices: 3.59 us -> 6.7 us  [shards(): one = lax.ppermute(features, 'rep', away[1])]
    ppermute x1, waiting for transfers between devices: 2.95 us -> 0.01 us  [shards(): ahead = lax.ppermute(one[:half], 'rep', away[1])]
    ppermute x1, starting transfers between devices: 3.92 us -> 6.01 us  [shards(): ahead = lax.ppermute(one[:half], 'rep', away[1])]
    ppermute x4 -> x3, starting transfers between devices: 10.4 us -> 12.1 us  [the longest x1 7.03 us: shards(): lax.ppermute(two, 'rep', sibling)]
  transfers between devices with their start and end apart: 12 -> 11, of which waited for: 5 -> 5; matrix products, arithmetic and copies ran while one was open for 3% -> 3% of each run, Pallas kernels for 14% -> 14%
where the time goes in v3:
time: 96.5 us; the launch traced here: 96 us
  starting transfers between devices  55.6 us (58%)
  Pallas kernels  23.1 us (24%)
  waiting for transfers between devices  13.2 us (14%)
  other arithmetic  2.84 us (3%)
  local copies, waits for them, and re-layouts  1 us (1%)
    pallas_call x3, Pallas kernels, aggregate(): pl.pallas_call(functools.partial(aggregate_kernel, sources, kinds, width,...  21.3 us
    ppermute x1, starting transfers between devices, shards(): upper = lax.ppermute(words, 'blk', down)  13.1 us
    ppermute x1, starting transfers between devices, shards(): from_above = lax.ppermute(for_lower, 'blk', down)  8.53 us
    ppermute x1, starting transfers between devices, shards(): lax.ppermute(two, 'rep', sibling)  7.03 us
    ppermute x1, starting transfers between devices, shards(): one = lax.ppermute(features, 'rep', away[1])  6.7 us
    ppermute x1, starting transfers between devices, shards(): ahead = lax.ppermute(one[:half], 'rep', away[1])  6.01 us
    ppermute x1, waiting for transfers between devices, shards(): lower = lax.ppermute(words, 'blk', up)  4.84 us
    ppermute x1, waiting for transfers between devices, shards(): from_below = lax.ppermute(for_upper, 'blk', up)  4.4 us
  transfers between devices with their start and end apart: 11, of which 5 were waited for; matrix products, arithmetic and copies ran while one was open for 3% of the time, Pallas kernels for 14%

profile of v3, /device:TPU:1, one launch (start us, length us, event | category | flops | bytes accessed | tf_op | source)
XLA Modules:
  0.0 96.0 jit_solution(754960771682687716)
XLA Ops:
  0.0 6.7 %collective-permute-start.1 = (bf16[1024,256]{1,0:T(8,128)(2,1)}, bf16[1024,256]{1,0:T(8,128)(2,1)S(1)}, u32[]{:S(2)}, u32[]{:S(2)}) collective-permute-start(bf16[1024,256]{1,0:T(8,128)(2,1)} %features_ref.1), channel_id=1, source_target_pairs={{0,6},{1,7},{2,0},{3,1},{4,2},{5,3},{6,4},{7,5},{8,14},{9,15},{10,... | collective-permute-start | bytes 1572872 | tf_op jit(solution)/shard_map/ppermute | solution.py:207
  6.7 1.9 %collective-permute-start.2 = (bf16[1024,256]{1,0:T(8,128)(2,1)}, bf16[1024,256]{1,0:T(8,128)(2,1)S(1)}, u32[]{:S(2)}, u32[]{:S(2)}) collective-permute-start(bf16[1024,256]{1,0:T(8,128)(2,1)} %features_ref.1), channel_id=1, source_target_pairs={{0,2},{1,3},{2,4},{3,5},{4,6},{5,7},{6,0},{7,1},{8,10},{9,11},{10,... | collective-permute-start | bytes 1572872 | tf_op jit(solution)/shard_map/ppermute | solution.py:208
  8.7 0.0 copy-start.5
  8.7 0.6 copy-done.5
  9.4 0.1 copy.8
  9.5 0.1 fusion.11
  9.6 0.1 select_select_fusion
  9.7 0.1 copy.12
  9.7 0.9 convert_reduce_fusion
  10.6 0.3 add_reduce_fusion
  11.0 1.2 %convert.10 = s16[8,44,4,128]{3,2,1,0:T(4,128)(2,1)S(1)} convert(s32[8,44,4,128]{3,2,1,0:T(4,128)} %param.8) | non-fusion elementwise | flops 180224 | bytes 1081344 | tf_op jit(solution)/shard_map/convert.5
  12.2 0.0 copy-start
  12.3 13.1 %collective-permute-start.5 = (s16[8,192,128]{2,1,0:T(8,128)(2,1)S(1)}, s16[8,192,128]{2,1,0:T(8,128)(2,1)S(1)}, u32[]{:S(2)}, u32[]{:S(2)}) collective-permute-start(s16[8,192,128]{2,1,0:T(8,128)(2,1)S(1)} %pad_add_fusion.refs_0_), channel_id=1, source_target_pairs={{8,0},{16,8},{24,16},{32,24},{40,32},{48,40},{56,48},{64,56},{72,6... | collective-permute-start | bytes 1179656 | tf_op jit(solution)/shard_map/ppermute | solution.py:212
  25.4 0.0 copy-done
  25.4 3.1 %collective-permute-start = (bf16[1024,256]{1,0:T(8,128)(2,1)S(1)}, bf16[1024,256]{1,0:T(8,128)(2,1)S(1)}, u32[]{:S(2)}, u32[]{:S(2)}) collective-permute-start(bf16[1024,256]{1,0:T(8,128)(2,1)S(1)} %copy-done), channel_id=1, source_target_pairs={{0,1},{1,0},{2,3},{3,2},{4,5},{5,4},{6,7},{7,6},{8,9},{9,8},{10,11... | collective-permute-start | bytes 1572872 | tf_op jit(solution)/shard_map/ppermute | solution.py:218
  28.5 1.9 %collective-permute-start.6 = (s16[8,192,128]{2,1,0:T(8,128)(2,1)S(1)}, s16[8,192,128]{2,1,0:T(8,128)(2,1)S(1)}, u32[]{:S(2)}, u32[]{:S(2)}) collective-permute-start(s16[8,192,128]{2,1,0:T(8,128)(2,1)S(1)} %pad_add_fusion.refs_0_), channel_id=1, source_target_pairs={{0,8},{8,16},{16,24},{24,32},{32,40},{40,48},{48,56},{56,64},{64,7... | collective-permute-start | bytes 1179656 | tf_op jit(solution)/shard_map/ppermute | solution.py:213
  30.5 0.0 collective-permute-done.1
  30.5 0.0 collective-permute-done.2
  30.6 1.9 %collective-permute-start.8 = (bf16[2048,256]{1,0:T(8,128)(2,1)S(1)}, bf16[2048,256]{1,0:T(8,128)(2,1)S(1)}, u32[]{:S(2)}, u32[]{:S(2)}) collective-permute-start(bf16[2048,256]{1,0:T(8,128)(2,1)S(1)} %constant_dynamic-update-slice_fusion.refs_4_.refs_3_), channel_id=1, source_target_pairs={{0,1},{1,0},{2,3},{3,2},{4,5},{5,4},{6,7},{7,6},{8,9},{9,8},{10,11... | collective-permute-start | bytes 3145736 | tf_op jit(solution)/shard_map/ppermute | solution.py:223
  32.5 6.0 %collective-permute-start.3 = (bf16[512,256]{1,0:T(8,128)(2,1)S(1)}, bf16[512,256]{1,0:T(8,128)(2,1)S(1)}, u32[]{:S(2)}, u32[]{:S(2)}) collective-permute-start(bf16[512,256]{1,0:T(8,128)(2,1)S(1)} %slice.8), channel_id=1, source_target_pairs={{0,6},{1,7},{2,0},{3,1},{4,2},{5,3},{6,4},{7,5},{8,14},{9,15},{10,... | collective-permute-start | bytes 786440 | tf_op jit(solution)/shard_map/ppermute | solution.py:215
  38.6 1.5 %collective-permute-done.5.refs_0_ = s16[8,192,128]{2,1,0:T(8,128)(2,1)S(1)} collective-permute-done((s16[8,192,128]{2,1,0:T(8,128)(2,1)S(1)}, s16[8,192,128]{2,1,0:T(8,128)(2,1)S(1)}, u32[]{:S(2)}, u32[]{:S(2)}) %collective-permute-start.5) | collective-permute-done | bytes 393248 | tf_op jit(solution)/shard_map/ppermute | solution.py:212
  40.1 3.3 %collective-permute-start.4 = (bf16[512,256]{1,0:T(8,128)(2,1)S(1)}, bf16[512,256]{1,0:T(8,128)(2,1)S(1)}, u32[]{:S(2)}, u32[]{:S(2)}) collective-permute-start(bf16[512,256]{1,0:T(8,128)(2,1)S(1)} %slice.9), channel_id=1, source_target_pairs={{0,2},{1,3},{2,4},{3,5},{4,6},{5,7},{6,0},{7,1},{8,10},{9,11},{10,... | collective-permute-start | bytes 786440 | tf_op jit(solution)/shard_map/ppermute | solution.py:216
  43.5 4.8 %collective-permute-done.6.refs_1_ = s16[8,192,128]{2,1,0:T(8,128)(2,1)S(1)} collective-permute-done((s16[8,192,128]{2,1,0:T(8,128)(2,1)S(1)}, s16[8,192,128]{2,1,0:T(8,128)(2,1)S(1)}, u32[]{:S(2)}, u32[]{:S(2)}) %collective-permute-start.6) | collective-permute-done | bytes 393248 | tf_op jit(solution)/shard_map/ppermute | solution.py:213
  48.3 0.0 collective-permute-done.refs_3_.refs_2_
  48.3 8.8 %aggregate.3 = (f32[8,128,256]{2,1,0:T(8,128)S(1)}, f32[8,128,256]{2,1,0:T(8,128)S(1)}) custom-call(s16[8,192,128]{2,1,0:T(8,128)(2,1)S(1)} %collective-permute-done.5.refs_0_, s16[8,192,128]{2,1,0:T(8,128)(2,1)S(1)} %collective-permute-done.6.refs_1_, bf16[1024,256]{1,0:T(8,128)(2,1)S(1)} %copy-done, ...), custom_call_target="tpu_custom_call" | custom-call | tf_op jit(solution)/shard_map/aggregate/pallas_call | solution.py:125
  57.1 0.0 collective-permute-done.3
  57.1 0.0 collective-permute-done.4
  57.2 0.0 copy-start.4
  57.2 7.0 %collective-permute-start.7 = (bf16[1024,256]{1,0:T(8,128)(2,1)S(1)}, bf16[1024,256]{1,0:T(8,128)(2,1)S(1)}, u32[]{:S(2)}, u32[]{:S(2)}) collective-permute-start(bf16[1024,256]{1,0:T(8,128)(2,1)S(1)} %constant_dynamic-update-slice_fusion.2.refs_4_.refs_2_), channel_id=1, source_target_pairs={{0,1},{1,0},{2,3},{3,2},{4,5},{5,4},{6,7},{7,6},{8,9},{9,8},{10,11... | collective-permute-start | bytes 1572872 | tf_op jit(solution)/shard_map/ppermute | solution.py:223
  64.3 1.5 %collective-permute-done.7.refs_5_.refs_3_ = bf16[1024,256]{1,0:T(8,128)(2,1)S(1)} collective-permute-done((bf16[1024,256]{1,0:T(8,128)(2,1)S(1)}, bf16[1024,256]{1,0:T(8,128)(2,1)S(1)}, u32[]{:S(2)}, u32[]{:S(2)}) %collective-permute-start.7) | collective-permute-done | bytes 524320 | tf_op jit(solution)/shard_map/ppermute | solution.py:223
  65.8 0.0 collective-permute-done.8.refs_6_.refs_4_
  65.8 7.7 %aggregate.5 = (s16[1040,256]{1,0:T(8,128)(2,1)S(1)}, s16[1040,256]{1,0:T(8,128)(2,1)S(1)}) custom-call(s16[8,192,128]{2,1,0:T(8,128)(2,1)S(1)} %collective-permute-done.5.refs_0_, s16[8,192,128]{2,1,0:T(8,128)(2,1)S(1)} %collective-permute-done.6.refs_1_, bf16[1024,256]{1,0:T(8,128)(2,1)S(1)} %constant_dynamic-update-slice_fusion.2.refs_4_.refs_2_, ...), custom_call_target="tpu_custom_call" | custom-call | tf_op jit(solution)/shard_map/aggregate/pallas_call | solution.py:125
  73.5 1.9 %collective-permute-start.9 = (s16[1040,256]{1,0:T(8,128)(2,1)S(1)}, s16[1040,256]{1,0:T(8,128)(2,1)S(1)}, u32[]{:S(2)}, u32[]{:S(2)}) collective-permute-start(s16[1040,256]{1,0:T(8,128)(2,1)S(1)} %get-tuple-element.20), channel_id=1, source_target_pairs={{0,8},{8,16},{16,24},{24,32},{32,40},{40,48},{48,56},{56,64},{64,7... | collective-permute-start | bytes 1597448 | tf_op jit(solution)/shard_map/ppermute | solution.py:225
  75.4 8.5 %collective-permute-start.10 = (s16[1040,256]{1,0:T(8,128)(2,1)S(1)}, s16[1040,256]{1,0:T(8,128)(2,1)S(1)}, u32[]{:S(2)}, u32[]{:S(2)}) collective-permute-start(s16[1040,256]{1,0:T(8,128)(2,1)S(1)} %get-tuple-element.21), channel_id=1, source_target_pairs={{8,0},{16,8},{24,16},{32,24},{40,32},{48,40},{56,48},{64,56},{72,6... | collective-permute-start | bytes 1597448 | tf_op jit(solution)/shard_map/ppermute | solution.py:226
  84.0 0.0 copy-done.4
  84.0 0.2 and_reduce_fusion
  84.2 0.0 copy-start.1
  84.2 0.0 copy-start.2
  84.2 4.8 %aggregate.4.own_ref = f32[8,128,256]{2,1,0:T(8,128)S(1)} custom-call(s16[8,192,128]{2,1,0:T(8,128)(2,1)S(1)} %pad_add_fusion.refs_0_, bf16[1024,256]{1,0:T(8,128)(2,1)S(1)} %copy-done, bf16[1024,256]{1,0:T(8,128)(2,1)S(1)} %collective-permute-done.refs_3_.refs_2_, bf16[2048,256]{1,0:T(8,128)(2,1)S(1)} %constant_dynamic-update-slice_fusion.refs_4_.refs_3_, ...), custom_call_target="tpu_custom_call" | custom-call | tf_op jit(solution)/shard_map/aggregate/pallas_call | solution.py:125
  89.0 0.0 copy-start.3
  89.0 4.4 %collective-permute-done.9.up_ref = s16[1040,256]{1,0:T(8,128)(2,1)S(1)} collective-permute-done((s16[1040,256]{1,0:T(8,128)(2,1)S(1)}, s16[1040,256]{1,0:T(8,128)(2,1)S(1)}, u32[]{:S(2)}, u32[]{:S(2)}) %collective-permute-start.9) | collective-permute-done | bytes 532512 | tf_op jit(solution)/shard_map/ppermute | solution.py:225
  93.4 0.9 collective-permute-done.10.down_ref
  94.3 0.0 copy-done.1
  94.3 0.0 copy-done.2
  94.3 0.0 copy-done.3
  94.3 1.7 %finish.1 = bf16[1024,256]{1,0:T(8,128)(2,1)} custom-call(f32[8,128,256]{2,1,0:T(8,128)S(1)} %aggregate.4.own_ref, s16[1040,256]{1,0:T(8,128)(2,1)S(1)} %collective-permute-done.9.up_ref, s16[1040,256]{1,0:T(8,128)(2,1)S(1)} %collective-permute-done.10.down_ref, f32[8,128]{1,0:T(8,128)S(1)} %convert_element_type.16.degree_ref, ...), custom_call_target="tpu_custom_call" | custom-call | flops 268435456 | bytes 4194304 | tf_op jit(solution)/shard_map/finish/pallas_call | solution.py:163
  (15 shorter events, 0.2 us)
Async XLA Ops:
  0.0 30.5 %collective-permute-start.1 = (bf16[1024,256]{1,0:T(8,128)(2,1)}, bf16[1024,256]{1,0:T(8,128)(2,1)S(1)}, u32[]{:S(2)}, u32[]{:S(2)}) collective-permute-start(bf16[1024,256]{1,0:T(8,128)(2,1)} %features_ref.1), channel_id=1, source_target_pairs={{0,6},{1,7},{2,0},{3,1},{4,2},{5,3},{6,4},{7,5},{8,14},{9,15},{10,... | collective-permute-start | bytes 1572872 | tf_op jit(solution)/shard_map/ppermute | solution.py:207
  6.7 23.8 %collective-permute-start.2 = (bf16[1024,256]{1,0:T(8,128)(2,1)}, bf16[1024,256]{1,0:T(8,128)(2,1)S(1)}, u32[]{:S(2)}, u32[]{:S(2)}) collective-permute-start(bf16[1024,256]{1,0:T(8,128)(2,1)} %features_ref.1), channel_id=1, source_target_pairs={{0,2},{1,3},{2,4},{3,5},{4,6},{5,7},{6,0},{7,1},{8,10},{9,11},{10,... | collective-permute-start | bytes 1572872 | tf_op jit(solution)/shard_map/ppermute | solution.py:208
  8.7 0.7 copy-start.5
  12.2 13.2 %copy-start = (bf16[1024,256]{1,0:T(8,128)(2,1)S(1)}, bf16[1024,256]{1,0:T(8,128)(2,1)}, u32[]{:S(2)}) copy-start(bf16[1024,256]{1,0:T(8,128)(2,1)} %features_ref.1) | copy-start | bytes 1572868
  12.3 27.9 %collective-permute-start.5 = (s16[8,192,128]{2,1,0:T(8,128)(2,1)S(1)}, s16[8,192,128]{2,1,0:T(8,128)(2,1)S(1)}, u32[]{:S(2)}, u32[]{:S(2)}) collective-permute-start(s16[8,192,128]{2,1,0:T(8,128)(2,1)S(1)} %pad_add_fusion.refs_0_), channel_id=1, source_target_pairs={{8,0},{16,8},{24,16},{32,24},{40,32},{48,40},{56,48},{64,56},{72,6... | collective-permute-start | bytes 1179656 | tf_op jit(solution)/shard_map/ppermute | solution.py:212
  25.4 22.9 %collective-permute-start = (bf16[1024,256]{1,0:T(8,128)(2,1)S(1)}, bf16[1024,256]{1,0:T(8,128)(2,1)S(1)}, u32[]{:S(2)}, u32[]{:S(2)}) collective-permute-start(bf16[1024,256]{1,0:T(8,128)(2,1)S(1)} %copy-done), channel_id=1, source_target_pairs={{0,1},{1,0},{2,3},{3,2},{4,5},{5,4},{6,7},{7,6},{8,9},{9,8},{10,11... | collective-permute-start | bytes 1572872 | tf_op jit(solution)/shard_map/ppermute | solution.py:218
  28.5 19.8 %collective-permute-start.6 = (s16[8,192,128]{2,1,0:T(8,128)(2,1)S(1)}, s16[8,192,128]{2,1,0:T(8,128)(2,1)S(1)}, u32[]{:S(2)}, u32[]{:S(2)}) collective-permute-start(s16[8,192,128]{2,1,0:T(8,128)(2,1)S(1)} %pad_add_fusion.refs_0_), channel_id=1, source_target_pairs={{0,8},{8,16},{16,24},{24,32},{32,40},{40,48},{48,56},{56,64},{64,7... | collective-permute-start | bytes 1179656 | tf_op jit(solution)/shard_map/ppermute | solution.py:213
  30.6 35.2 %collective-permute-start.8 = (bf16[2048,256]{1,0:T(8,128)(2,1)S(1)}, bf16[2048,256]{1,0:T(8,128)(2,1)S(1)}, u32[]{:S(2)}, u32[]{:S(2)}) collective-permute-start(bf16[2048,256]{1,0:T(8,128)(2,1)S(1)} %constant_dynamic-update-slice_fusion.refs_4_.refs_3_), channel_id=1, source_target_pairs={{0,1},{1,0},{2,3},{3,2},{4,5},{5,4},{6,7},{7,6},{8,9},{9,8},{10,11... | collective-permute-start | bytes 3145736 | tf_op jit(solution)/shard_map/ppermute | solution.py:223
  32.5 24.6 %collective-permute-start.3 = (bf16[512,256]{1,0:T(8,128)(2,1)S(1)}, bf16[512,256]{1,0:T(8,128)(2,1)S(1)}, u32[]{:S(2)}, u32[]{:S(2)}) collective-permute-start(bf16[512,256]{1,0:T(8,128)(2,1)S(1)} %slice.8), channel_id=1, source_target_pairs={{0,6},{1,7},{2,0},{3,1},{4,2},{5,3},{6,4},{7,5},{8,14},{9,15},{10,... | collective-permute-start | bytes 786440 | tf_op jit(solution)/shard_map/ppermute | solution.py:215
  40.1 17.0 %collective-permute-start.4 = (bf16[512,256]{1,0:T(8,128)(2,1)S(1)}, bf16[512,256]{1,0:T(8,128)(2,1)S(1)}, u32[]{:S(2)}, u32[]{:S(2)}) collective-permute-start(bf16[512,256]{1,0:T(8,128)(2,1)S(1)} %slice.9), channel_id=1, source_target_pairs={{0,2},{1,3},{2,4},{3,5},{4,6},{5,7},{6,0},{7,1},{8,10},{9,11},{10,... | collective-permute-start | bytes 786440 | tf_op jit(solution)/shard_map/ppermute | solution.py:216
  57.2 26.8 %copy-start.4 = (s32[8,44,4,128]{3,2,1,0:T(4,128)S(1)}, s32[8,44,4,128]{3,2,1,0:T(4,128)}, u32[]{:S(2)}) copy-start(s32[8,44,4,128]{3,2,1,0:T(4,128)} %param.8) | copy-start | bytes 2162692
  57.2 8.6 %collective-permute-start.7 = (bf16[1024,256]{1,0:T(8,128)(2,1)S(1)}, bf16[1024,256]{1,0:T(8,128)(2,1)S(1)}, u32[]{:S(2)}, u32[]{:S(2)}) collective-permute-start(bf16[1024,256]{1,0:T(8,128)(2,1)S(1)} %constant_dynamic-update-slice_fusion.2.refs_4_.refs_2_), channel_id=1, source_target_pairs={{0,1},{1,0},{2,3},{3,2},{4,5},{5,4},{6,7},{7,6},{8,9},{9,8},{10,11... | collective-permute-start | bytes 1572872 | tf_op jit(solution)/shard_map/ppermute | solution.py:223
  73.5 19.9 %collective-permute-start.9 = (s16[1040,256]{1,0:T(8,128)(2,1)S(1)}, s16[1040,256]{1,0:T(8,128)(2,1)S(1)}, u32[]{:S(2)}, u32[]{:S(2)}) collective-permute-start(s16[1040,256]{1,0:T(8,128)(2,1)S(1)} %get-tuple-element.20), channel_id=1, source_target_pairs={{0,8},{8,16},{16,24},{24,32},{32,40},{40,48},{48,56},{56,64},{64,7... | collective-permute-start | bytes 1597448 | tf_op jit(solution)/shard_map/ppermute | solution.py:225
  75.4 18.8 %collective-permute-start.10 = (s16[1040,256]{1,0:T(8,128)(2,1)S(1)}, s16[1040,256]{1,0:T(8,128)(2,1)S(1)}, u32[]{:S(2)}, u32[]{:S(2)}) collective-permute-start(s16[1040,256]{1,0:T(8,128)(2,1)S(1)} %get-tuple-element.21), channel_id=1, source_target_pairs={{8,0},{16,8},{24,16},{32,24},{40,32},{48,40},{56,48},{64,56},{72,6... | collective-permute-start | bytes 1597448 | tf_op jit(solution)/shard_map/ppermute | solution.py:226
  84.2 10.1 %copy-start.1 = (bf16[256,256]{1,0:T(8,128)(2,1)S(1)}, bf16[256,256]{1,0:T(8,128)(2,1)}, u32[]{:S(2)}) copy-start(bf16[256,256]{1,0:T(8,128)(2,1)} %self_ref.1) | copy-start | bytes 393220
  84.2 10.1 %copy-start.2 = (bf16[256,256]{1,0:T(8,128)(2,1)S(1)}, bf16[256,256]{1,0:T(8,128)(2,1)}, u32[]{:S(2)}) copy-start(bf16[256,256]{1,0:T(8,128)(2,1)} %neigh_ref.1) | copy-start | bytes 393220
  89.0 5.3 %copy-start.3 = (f32[256]{0:T(256)S(1)}, f32[256]{0:T(256)}, u32[]{:S(2)}) copy-start(f32[256]{0:T(256)} %param.11) | copy-start | bytes 3076

commit v4 on v3

--- a/solution.py
+++ b/solution.py
@@ -53,26 +53,28 @@
     for source in range(sources):
         for r in range(ROWS):
             noted[source, r] = words[source][r, CODED:, :].astype(jnp.int32)
-    scalars = pltpu.make_async_copy(noted.at[:, :, pl.ds(0, 8)], lists_ref, sems.at[pieces])
-    scalars.start()
+    scalars = [
+        pltpu.make_async_copy(noted.at[source, :, kinds[source]], lists_ref.at[source], sems.at[pieces + source])
+        for source in range(sources)
+    ]
+    for copy in scalars:
+        copy.start()
     for source in range(sources):
         for r in range(ROWS):
             coded[source, r] = words[source][r, :CODED, :].astype(jnp.int32)
-    scalars.wait()
-    for copy in copies:
+    for copy in scalars + copies:
         copy.wait()
 
     for source in range(sources):
         out_ref = totals[source]
-        kind = kinds[source]
 
         def chunk(r, c):
-            count = lists_ref[source, r, kind, BS - 1]
+            count = lists_ref[source, r, BS - 1]
             left = []
             right = []
             for u in range(width):
                 entry = c * width + u
-                code = lists_ref[source, r, kind, entry]
+                code = lists_ref[source, r, entry]
                 at = pl.multiple_of(lax.shift_right_logical(code, 7) * 4, 4)
                 some = jnp.where(entry < count, coded[source, r, pl.ds(at, 4), :], 0)
                 left.append(unpack(some))
@@ -93,7 +95,7 @@
                     out_ref[r] += chunk(r, c)
                     return 0
 
-                lax.fori_loop(1, (lists_ref[source, r, kind, BS - 1] + width - 1) // width, more, 0)
+                lax.fori_loop(1, (lists_ref[source, r, BS - 1] + width - 1) // width, more, 0)
             return 0
 
         lax.fori_loop(0, ROWS // together, rows, 0)
@@ -132,8 +134,8 @@
             pltpu.VMEM((sum(part.shape[0] for part in parts), WIDTH), jnp.bfloat16),
             pltpu.VMEM((sources, ROWS, CODED, BS), jnp.int32),
             pltpu.VMEM((sources, ROWS, 16, BS), jnp.int32),
-            pltpu.SMEM((sources, ROWS, 8, BS), jnp.int32),
-            pltpu.SemaphoreType.DMA((pieces + 1,)),
+            pltpu.SMEM((sources, ROWS, BS), jnp.int32),
+            pltpu.SemaphoreType.DMA((pieces + sources,)),
         ],
         compiler_params=pltpu.CompilerParams(vmem_limit_bytes=40 * 2**20),
         cost_estimate=pl.CostEstimate(flops=0, bytes_accessed=0, transcendentals=0),
@@ -217,17 +219,17 @@
     both = jnp.concatenate([one, three], axis=0)
     sib_own = lax.ppermute(features, "rep", sibling)
     early = [features, sib_own, both]
-    sums = aggregate([upper, lower], (0, 2), early, 10, 2)
+    sums = aggregate([upper, lower], (0, 2), early, 8, 8)
     ahead, behind, *sums = lax.optimization_barrier((ahead, behind, *sums))
     two = jnp.concatenate([ahead, behind], axis=0)
     late = [two, lax.ppermute(two, "rep", sibling), lax.ppermute(both, "rep", sibling)]
-    for_upper, for_lower = aggregate([upper, lower], (1, 3), late, 10, 2, sums, True)
+    for_upper, for_lower = aggregate([upper, lower], (1, 3), late, 10, 4, sums, True)
     from_below = lax.ppermute(for_upper, "blk", up)
     from_above = lax.ppermute(for_lower, "blk", down)
     pieces = early + late
     coded, _ = lax.optimization_barrier((adjacency, for_upper))
     degree = jnp.sum(jnp.bitwise_and(coded, 3), axis=(1, 2)).astype(jnp.float32)
-    (mine,) = aggregate([words], (4,), pieces, 16, 2)
+    (mine,) = aggregate([words], (4,), pieces, 16, 8)
     return finish(mine, from_below, from_above, degree, features, w_self, w_neigh, bias)
 
 

time: 96.5 us -> 95.1 us (0.985)
  Pallas kernels: 23.1 us -> 18.2 us
  waiting for transfers between devices: 13.2 us -> 17.1 us
    pallas_call x3, Pallas kernels: 21.3 us -> 16.5 us  [aggregate(): pl.pallas_call(functools.partial(aggregate_kernel, sources, kinds, width,...]
    ppermute x1, waiting for transfers between devices: 0.01 us -> 3.22 us  [shards(): behind = lax.ppermute(three[half:], 'rep', away[3])]
    ppermute x1, starting transfers between devices: 7.03 us -> 5.18 us  [shards(): lax.ppermute(two, 'rep', sibling)]
    ppermute x1, starting transfers between devices: 8.53 us -> 10.2 us  [shards(): from_above = lax.ppermute(for_lower, 'blk', down)]
  transfers between devices with their start and end apart: 11 -> 11, of which waited for: 5 -> 6; matrix products, arithmetic and copies ran while one was open for 3% -> 3% of each run, Pallas kernels for 14% -> 11%
where the time goes in v4:
time: 95.1 us; the launch traced here: 94.8 us
  starting transfers between devices  55.3 us (58%)
  Pallas kernels  18.2 us (19%)
  waiting for transfers between devices  17.1 us (18%)
  other arithmetic  2.84 us (3%)
  local copies, waits for them, and re-layouts  1 us (1%)
    pallas_call x3, Pallas kernels, aggregate(): pl.pallas_call(functools.partial(aggregate_kernel, sources, kinds, width,...  16.5 us
    ppermute x1, starting transfers between devices, shards(): upper = lax.ppermute(words, 'blk', down)  13.1 us
    ppermute x1, starting transfers between devices, shards(): from_above = lax.ppermute(for_lower, 'blk', down)  10.2 us
    ppermute x1, starting transfers between devices, shards(): one = lax.ppermute(features, 'rep', away[1])  6.7 us
    ppermute x1, starting transfers between devices, shards(): ahead = lax.ppermute(one[:half], 'rep', away[1])  6.01 us
    ppermute x1, waiting for transfers between devices, shards(): from_below = lax.ppermute(for_upper, 'blk', up)  5.28 us
    ppermute x1, starting transfers between devices, shards(): lax.ppermute(two, 'rep', sibling)  5.18 us
    ppermute x1, waiting for transfers between devices, shards(): lower = lax.ppermute(words, 'blk', up)  4.84 us
  transfers between devices with their start and end apart: 11, of which 6 were waited for; matrix products, arithmetic and copies ran while one was open for 3% of the time, Pallas kernels for 11%

profile of v4, /device:TPU:1, one launch (start us, length us, event | category | flops | bytes accessed | tf_op | source)
XLA Modules:
  0.0 94.8 jit_solution(5817148392186902632)
XLA Ops:
  0.0 6.7 %collective-permute-start.1 = (bf16[1024,256]{1,0:T(8,128)(2,1)}, bf16[1024,256]{1,0:T(8,128)(2,1)S(1)}, u32[]{:S(2)}, u32[]{:S(2)}) collective-permute-start(bf16[1024,256]{1,0:T(8,128)(2,1)} %features_ref.1), channel_id=1, source_target_pairs={{0,6},{1,7},{2,0},{3,1},{4,2},{5,3},{6,4},{7,5},{8,14},{9,15},{10,... | collective-permute-start | bytes 1572872 | tf_op jit(solution)/shard_map/ppermute | solution.py:209
  6.7 1.9 %collective-permute-start.2 = (bf16[1024,256]{1,0:T(8,128)(2,1)}, bf16[1024,256]{1,0:T(8,128)(2,1)S(1)}, u32[]{:S(2)}, u32[]{:S(2)}) collective-permute-start(bf16[1024,256]{1,0:T(8,128)(2,1)} %features_ref.1), channel_id=1, source_target_pairs={{0,2},{1,3},{2,4},{3,5},{4,6},{5,7},{6,0},{7,1},{8,10},{9,11},{10,... | collective-permute-start | bytes 1572872 | tf_op jit(solution)/shard_map/ppermute | solution.py:210
  8.7 0.0 copy-start.5
  8.7 0.6 copy-done.5
  9.4 0.1 copy.8
  9.5 0.1 fusion.11
  9.6 0.1 select_select_fusion
  9.7 0.1 copy.12
  9.7 0.9 convert_reduce_fusion
  10.6 0.3 add_reduce_fusion
  11.0 1.2 %convert.10 = s16[8,44,4,128]{3,2,1,0:T(4,128)(2,1)S(1)} convert(s32[8,44,4,128]{3,2,1,0:T(4,128)} %param.8) | non-fusion elementwise | flops 180224 | bytes 1081344 | tf_op jit(solution)/shard_map/convert.5
  12.2 0.0 copy-start
  12.3 13.1 %collective-permute-start.5 = (s16[8,192,128]{2,1,0:T(8,128)(2,1)S(1)}, s16[8,192,128]{2,1,0:T(8,128)(2,1)S(1)}, u32[]{:S(2)}, u32[]{:S(2)}) collective-permute-start(s16[8,192,128]{2,1,0:T(8,128)(2,1)S(1)} %pad_add_fusion.refs_0_), channel_id=1, source_target_pairs={{8,0},{16,8},{24,16},{32,24},{40,32},{48,40},{56,48},{64,56},{72,6... | collective-permute-start | bytes 1179656 | tf_op jit(solution)/shard_map/ppermute | solution.py:214
  25.4 0.0 copy-done
  25.4 3.1 %collective-permute-start = (bf16[1024,256]{1,0:T(8,128)(2,1)S(1)}, bf16[1024,256]{1,0:T(8,128)(2,1)S(1)}, u32[]{:S(2)}, u32[]{:S(2)}) collective-permute-start(bf16[1024,256]{1,0:T(8,128)(2,1)S(1)} %copy-done), channel_id=1, source_target_pairs={{0,1},{1,0},{2,3},{3,2},{4,5},{5,4},{6,7},{7,6},{8,9},{9,8},{10,11... | collective-permute-start | bytes 1572872 | tf_op jit(solution)/shard_map/ppermute | solution.py:220
  28.5 1.9 %collective-permute-start.6 = (s16[8,192,128]{2,1,0:T(8,128)(2,1)S(1)}, s16[8,192,128]{2,1,0:T(8,128)(2,1)S(1)}, u32[]{:S(2)}, u32[]{:S(2)}) collective-permute-start(s16[8,192,128]{2,1,0:T(8,128)(2,1)S(1)} %pad_add_fusion.refs_0_), channel_id=1, source_target_pairs={{0,8},{8,16},{16,24},{24,32},{32,40},{40,48},{48,56},{56,64},{64,7... | collective-permute-start | bytes 1179656 | tf_op jit(solution)/shard_map/ppermute | solution.py:215
  30.5 0.0 collective-permute-done.1
  30.5 0.0 collective-permute-done.2
  30.6 1.9 %collective-permute-start.8 = (bf16[2048,256]{1,0:T(8,128)(2,1)S(1)}, bf16[2048,256]{1,0:T(8,128)(2,1)S(1)}, u32[]{:S(2)}, u32[]{:S(2)}) collective-permute-start(bf16[2048,256]{1,0:T(8,128)(2,1)S(1)} %constant_dynamic-update-slice_fusion.refs_4_.refs_3_), channel_id=1, source_target_pairs={{0,1},{1,0},{2,3},{3,2},{4,5},{5,4},{6,7},{7,6},{8,9},{9,8},{10,11... | collective-permute-start | bytes 3145736 | tf_op jit(solution)/shard_map/ppermute | solution.py:225
  32.5 6.0 %collective-permute-start.3 = (bf16[512,256]{1,0:T(8,128)(2,1)S(1)}, bf16[512,256]{1,0:T(8,128)(2,1)S(1)}, u32[]{:S(2)}, u32[]{:S(2)}) collective-permute-start(bf16[512,256]{1,0:T(8,128)(2,1)S(1)} %slice.8), channel_id=1, source_target_pairs={{0,6},{1,7},{2,0},{3,1},{4,2},{5,3},{6,4},{7,5},{8,14},{9,15},{10,... | collective-permute-start | bytes 786440 | tf_op jit(solution)/shard_map/ppermute | solution.py:217
  38.6 1.5 %collective-permute-done.5.refs_0_ = s16[8,192,128]{2,1,0:T(8,128)(2,1)S(1)} collective-permute-done((s16[8,192,128]{2,1,0:T(8,128)(2,1)S(1)}, s16[8,192,128]{2,1,0:T(8,128)(2,1)S(1)}, u32[]{:S(2)}, u32[]{:S(2)}) %collective-permute-start.5) | collective-permute-done | bytes 393248 | tf_op jit(solution)/shard_map/ppermute | solution.py:214
  40.1 3.3 %collective-permute-start.4 = (bf16[512,256]{1,0:T(8,128)(2,1)S(1)}, bf16[512,256]{1,0:T(8,128)(2,1)S(1)}, u32[]{:S(2)}, u32[]{:S(2)}) collective-permute-start(bf16[512,256]{1,0:T(8,128)(2,1)S(1)} %slice.9), channel_id=1, source_target_pairs={{0,2},{1,3},{2,4},{3,5},{4,6},{5,7},{6,0},{7,1},{8,10},{9,11},{10,... | collective-permute-start | bytes 786440 | tf_op jit(solution)/shard_map/ppermute | solution.py:218
  43.5 4.8 %collective-permute-done.6.refs_1_ = s16[8,192,128]{2,1,0:T(8,128)(2,1)S(1)} collective-permute-done((s16[8,192,128]{2,1,0:T(8,128)(2,1)S(1)}, s16[8,192,128]{2,1,0:T(8,128)(2,1)S(1)}, u32[]{:S(2)}, u32[]{:S(2)}) %collective-permute-start.6) | collective-permute-done | bytes 393248 | tf_op jit(solution)/shard_map/ppermute | solution.py:215
  48.3 0.0 collective-permute-done.refs_3_.refs_2_
  48.3 5.3 %aggregate.3 = (f32[8,128,256]{2,1,0:T(8,128)S(1)}, f32[8,128,256]{2,1,0:T(8,128)S(1)}) custom-call(s16[8,192,128]{2,1,0:T(8,128)(2,1)S(1)} %collective-permute-done.5.refs_0_, s16[8,192,128]{2,1,0:T(8,128)(2,1)S(1)} %collective-permute-done.6.refs_1_, bf16[1024,256]{1,0:T(8,128)(2,1)S(1)} %copy-done, ...), custom_call_target="tpu_custom_call" | custom-call | tf_op jit(solution)/shard_map/aggregate/pallas_call | solution.py:127
  53.6 0.0 collective-permute-done.3
  53.6 3.2 %collective-permute-done.4 = bf16[512,256]{1,0:T(8,128)(2,1)S(1)} collective-permute-done((bf16[512,256]{1,0:T(8,128)(2,1)S(1)}, bf16[512,256]{1,0:T(8,128)(2,1)S(1)}, u32[]{:S(2)}, u32[]{:S(2)}) %collective-permute-start.4) | collective-permute-done | bytes 262176 | tf_op jit(solution)/shard_map/ppermute | solution.py:218
  56.9 0.0 copy-start.4
  56.9 5.2 %collective-permute-start.7 = (bf16[1024,256]{1,0:T(8,128)(2,1)S(1)}, bf16[1024,256]{1,0:T(8,128)(2,1)S(1)}, u32[]{:S(2)}, u32[]{:S(2)}) collective-permute-start(bf16[1024,256]{1,0:T(8,128)(2,1)S(1)} %constant_dynamic-update-slice_fusion.2.refs_4_.refs_2_), channel_id=1, source_target_pairs={{0,1},{1,0},{2,3},{3,2},{4,5},{5,4},{6,7},{7,6},{8,9},{9,8},{10,11... | collective-permute-start | bytes 1572872 | tf_op jit(solution)/shard_map/ppermute | solution.py:225
  62.1 1.3 %collective-permute-done.7.refs_5_.refs_3_ = bf16[1024,256]{1,0:T(8,128)(2,1)S(1)} collective-permute-done((bf16[1024,256]{1,0:T(8,128)(2,1)S(1)}, bf16[1024,256]{1,0:T(8,128)(2,1)S(1)}, u32[]{:S(2)}, u32[]{:S(2)}) %collective-permute-start.7) | collective-permute-done | bytes 524320 | tf_op jit(solution)/shard_map/ppermute | solution.py:225
  63.4 0.0 collective-permute-done.8.refs_6_.refs_4_
  63.4 6.5 %aggregate.5 = (s16[1040,256]{1,0:T(8,128)(2,1)S(1)}, s16[1040,256]{1,0:T(8,128)(2,1)S(1)}) custom-call(s16[8,192,128]{2,1,0:T(8,128)(2,1)S(1)} %collective-permute-done.5.refs_0_, s16[8,192,128]{2,1,0:T(8,128)(2,1)S(1)} %collective-permute-done.6.refs_1_, bf16[1024,256]{1,0:T(8,128)(2,1)S(1)} %constant_dynamic-update-slice_fusion.2.refs_4_.refs_2_, ...), custom_call_target="tpu_custom_call" | custom-call | tf_op jit(solution)/shard_map/aggregate/pallas_call | solution.py:127
  69.9 1.9 %collective-permute-start.9 = (s16[1040,256]{1,0:T(8,128)(2,1)S(1)}, s16[1040,256]{1,0:T(8,128)(2,1)S(1)}, u32[]{:S(2)}, u32[]{:S(2)}) collective-permute-start(s16[1040,256]{1,0:T(8,128)(2,1)S(1)} %get-tuple-element.20), channel_id=1, source_target_pairs={{0,8},{8,16},{16,24},{24,32},{32,40},{40,48},{48,56},{56,64},{64,7... | collective-permute-start | bytes 1597448 | tf_op jit(solution)/shard_map/ppermute | solution.py:227
  71.8 10.2 %collective-permute-start.10 = (s16[1040,256]{1,0:T(8,128)(2,1)S(1)}, s16[1040,256]{1,0:T(8,128)(2,1)S(1)}, u32[]{:S(2)}, u32[]{:S(2)}) collective-permute-start(s16[1040,256]{1,0:T(8,128)(2,1)S(1)} %get-tuple-element.21), channel_id=1, source_target_pairs={{8,0},{16,8},{24,16},{32,24},{40,32},{48,40},{56,48},{64,56},{72,6... | collective-permute-start | bytes 1597448 | tf_op jit(solution)/shard_map/ppermute | solution.py:228
  82.0 0.0 copy-done.4
  82.0 0.2 and_reduce_fusion
  82.2 0.0 copy-start.1
  82.2 0.0 copy-start.2
  82.2 4.7 %aggregate.4.own_ref = f32[8,128,256]{2,1,0:T(8,128)S(1)} custom-call(s16[8,192,128]{2,1,0:T(8,128)(2,1)S(1)} %pad_add_fusion.refs_0_, bf16[1024,256]{1,0:T(8,128)(2,1)S(1)} %copy-done, bf16[1024,256]{1,0:T(8,128)(2,1)S(1)} %collective-permute-done.refs_3_.refs_2_, bf16[2048,256]{1,0:T(8,128)(2,1)S(1)} %constant_dynamic-update-slice_fusion.refs_4_.refs_3_, ...), custom_call_target="tpu_custom_call" | custom-call | tf_op jit(solution)/shard_map/aggregate/pallas_call | solution.py:127
  86.9 0.0 copy-start.3
  86.9 5.3 %collective-permute-done.9.up_ref = s16[1040,256]{1,0:T(8,128)(2,1)S(1)} collective-permute-done((s16[1040,256]{1,0:T(8,128)(2,1)S(1)}, s16[1040,256]{1,0:T(8,128)(2,1)S(1)}, u32[]{:S(2)}, u32[]{:S(2)}) %collective-permute-start.9) | collective-permute-done | bytes 532512 | tf_op jit(solution)/shard_map/ppermute | solution.py:227
  92.2 0.9 collective-permute-done.10.down_ref
  93.1 0.0 copy-done.1
  93.1 0.0 copy-done.2
  93.1 0.0 copy-done.3
  93.1 1.7 %finish.1 = bf16[1024,256]{1,0:T(8,128)(2,1)} custom-call(f32[8,128,256]{2,1,0:T(8,128)S(1)} %aggregate.4.own_ref, s16[1040,256]{1,0:T(8,128)(2,1)S(1)} %collective-permute-done.9.up_ref, s16[1040,256]{1,0:T(8,128)(2,1)S(1)} %collective-permute-done.10.down_ref, f32[8,128]{1,0:T(8,128)S(1)} %convert_element_type.16.degree_ref, ...), custom_call_target="tpu_custom_call" | custom-call | flops 268435456 | bytes 4194304 | tf_op jit(solution)/shard_map/finish/pallas_call | solution.py:165
  (15 shorter events, 0.2 us)
Async XLA Ops:
  0.0 30.5 %collective-permute-start.1 = (bf16[1024,256]{1,0:T(8,128)(2,1)}, bf16[1024,256]{1,0:T(8,128)(2,1)S(1)}, u32[]{:S(2)}, u32[]{:S(2)}) collective-permute-start(bf16[1024,256]{1,0:T(8,128)(2,1)} %features_ref.1), channel_id=1, source_target_pairs={{0,6},{1,7},{2,0},{3,1},{4,2},{5,3},{6,4},{7,5},{8,14},{9,15},{10,... | collective-permute-start | bytes 1572872 | tf_op jit(solution)/shard_map/ppermute | solution.py:209
  6.7 23.8 %collective-permute-start.2 = (bf16[1024,256]{1,0:T(8,128)(2,1)}, bf16[1024,256]{1,0:T(8,128)(2,1)S(1)}, u32[]{:S(2)}, u32[]{:S(2)}) collective-permute-start(bf16[1024,256]{1,0:T(8,128)(2,1)} %features_ref.1), channel_id=1, source_target_pairs={{0,2},{1,3},{2,4},{3,5},{4,6},{5,7},{6,0},{7,1},{8,10},{9,11},{10,... | collective-permute-start | bytes 1572872 | tf_op jit(solution)/shard_map/ppermute | solution.py:210
  8.7 0.7 copy-start.5
  12.2 13.2 %copy-start = (bf16[1024,256]{1,0:T(8,128)(2,1)S(1)}, bf16[1024,256]{1,0:T(8,128)(2,1)}, u32[]{:S(2)}) copy-start(bf16[1024,256]{1,0:T(8,128)(2,1)} %features_ref.1) | copy-start | bytes 1572868
  12.3 27.9 %collective-permute-start.5 = (s16[8,192,128]{2,1,0:T(8,128)(2,1)S(1)}, s16[8,192,128]{2,1,0:T(8,128)(2,1)S(1)}, u32[]{:S(2)}, u32[]{:S(2)}) collective-permute-start(s16[8,192,128]{2,1,0:T(8,128)(2,1)S(1)} %pad_add_fusion.refs_0_), channel_id=1, source_target_pairs={{8,0},{16,8},{24,16},{32,24},{40,32},{48,40},{56,48},{64,56},{72,6... | collective-permute-start | bytes 1179656 | tf_op jit(solution)/shard_map/ppermute | solution.py:214
  25.4 22.9 %collective-permute-start = (bf16[1024,256]{1,0:T(8,128)(2,1)S(1)}, bf16[1024,256]{1,0:T(8,128)(2,1)S(1)}, u32[]{:S(2)}, u32[]{:S(2)}) collective-permute-start(bf16[1024,256]{1,0:T(8,128)(2,1)S(1)} %copy-done), channel_id=1, source_target_pairs={{0,1},{1,0},{2,3},{3,2},{4,5},{5,4},{6,7},{7,6},{8,9},{9,8},{10,11... | collective-permute-start | bytes 1572872 | tf_op jit(solution)/shard_map/ppermute | solution.py:220
  28.5 19.8 %collective-permute-start.6 = (s16[8,192,128]{2,1,0:T(8,128)(2,1)S(1)}, s16[8,192,128]{2,1,0:T(8,128)(2,1)S(1)}, u32[]{:S(2)}, u32[]{:S(2)}) collective-permute-start(s16[8,192,128]{2,1,0:T(8,128)(2,1)S(1)} %pad_add_fusion.refs_0_), channel_id=1, source_target_pairs={{0,8},{8,16},{16,24},{24,32},{32,40},{40,48},{48,56},{56,64},{64,7... | collective-permute-start | bytes 1179656 | tf_op jit(solution)/shard_map/ppermute | solution.py:215
  30.6 32.8 %collective-permute-start.8 = (bf16[2048,256]{1,0:T(8,128)(2,1)S(1)}, bf16[2048,256]{1,0:T(8,128)(2,1)S(1)}, u32[]{:S(2)}, u32[]{:S(2)}) collective-permute-start(bf16[2048,256]{1,0:T(8,128)(2,1)S(1)} %constant_dynamic-update-slice_fusion.refs_4_.refs_3_), channel_id=1, source_target_pairs={{0,1},{1,0},{2,3},{3,2},{4,5},{5,4},{6,7},{7,6},{8,9},{9,8},{10,11... | collective-permute-start | bytes 3145736 | tf_op jit(solution)/shard_map/ppermute | solution.py:225
  32.5 21.1 %collective-permute-start.3 = (bf16[512,256]{1,0:T(8,128)(2,1)S(1)}, bf16[512,256]{1,0:T(8,128)(2,1)S(1)}, u32[]{:S(2)}, u32[]{:S(2)}) collective-permute-start(bf16[512,256]{1,0:T(8,128)(2,1)S(1)} %slice.8), channel_id=1, source_target_pairs={{0,6},{1,7},{2,0},{3,1},{4,2},{5,3},{6,4},{7,5},{8,14},{9,15},{10,... | collective-permute-start | bytes 786440 | tf_op jit(solution)/shard_map/ppermute | solution.py:217
  40.1 16.7 %collective-permute-start.4 = (bf16[512,256]{1,0:T(8,128)(2,1)S(1)}, bf16[512,256]{1,0:T(8,128)(2,1)S(1)}, u32[]{:S(2)}, u32[]{:S(2)}) collective-permute-start(bf16[512,256]{1,0:T(8,128)(2,1)S(1)} %slice.9), channel_id=1, source_target_pairs={{0,2},{1,3},{2,4},{3,5},{4,6},{5,7},{6,0},{7,1},{8,10},{9,11},{10,... | collective-permute-start | bytes 786440 | tf_op jit(solution)/shard_map/ppermute | solution.py:218
  56.9 25.1 %copy-start.4 = (s32[8,44,4,128]{3,2,1,0:T(4,128)S(1)}, s32[8,44,4,128]{3,2,1,0:T(4,128)}, u32[]{:S(2)}) copy-start(s32[8,44,4,128]{3,2,1,0:T(4,128)} %param.8) | copy-start | bytes 2162692
  56.9 6.5 %collective-permute-start.7 = (bf16[1024,256]{1,0:T(8,128)(2,1)S(1)}, bf16[1024,256]{1,0:T(8,128)(2,1)S(1)}, u32[]{:S(2)}, u32[]{:S(2)}) collective-permute-start(bf16[1024,256]{1,0:T(8,128)(2,1)S(1)} %constant_dynamic-update-slice_fusion.2.refs_4_.refs_2_), channel_id=1, source_target_pairs={{0,1},{1,0},{2,3},{3,2},{4,5},{5,4},{6,7},{7,6},{8,9},{9,8},{10,11... | collective-permute-start | bytes 1572872 | tf_op jit(solution)/shard_map/ppermute | solution.py:225
  69.9 22.3 %collective-permute-start.9 = (s16[1040,256]{1,0:T(8,128)(2,1)S(1)}, s16[1040,256]{1,0:T(8,128)(2,1)S(1)}, u32[]{:S(2)}, u32[]{:S(2)}) collective-permute-start(s16[1040,256]{1,0:T(8,128)(2,1)S(1)} %get-tuple-element.20), channel_id=1, source_target_pairs={{0,8},{8,16},{16,24},{24,32},{32,40},{40,48},{48,56},{56,64},{64,7... | collective-permute-start | bytes 1597448 | tf_op jit(solution)/shard_map/ppermute | solution.py:227
  71.8 21.3 %collective-permute-start.10 = (s16[1040,256]{1,0:T(8,128)(2,1)S(1)}, s16[1040,256]{1,0:T(8,128)(2,1)S(1)}, u32[]{:S(2)}, u32[]{:S(2)}) collective-permute-start(s16[1040,256]{1,0:T(8,128)(2,1)S(1)} %get-tuple-element.21), channel_id=1, source_target_pairs={{8,0},{16,8},{24,16},{32,24},{40,32},{48,40},{56,48},{64,56},{72,6... | collective-permute-start | bytes 1597448 | tf_op jit(solution)/shard_map/ppermute | solution.py:228
  82.2 10.9 %copy-start.1 = (bf16[256,256]{1,0:T(8,128)(2,1)S(1)}, bf16[256,256]{1,0:T(8,128)(2,1)}, u32[]{:S(2)}) copy-start(bf16[256,256]{1,0:T(8,128)(2,1)} %self_ref.1) | copy-start | bytes 393220
  82.2 10.9 %copy-start.2 = (bf16[256,256]{1,0:T(8,128)(2,1)S(1)}, bf16[256,256]{1,0:T(8,128)(2,1)}, u32[]{:S(2)}) copy-start(bf16[256,256]{1,0:T(8,128)(2,1)} %neigh_ref.1) | copy-start | bytes 393220
  86.9 6.2 %copy-start.3 = (f32[256]{0:T(256)S(1)}, f32[256]{0:T(256)}, u32[]{:S(2)}) copy-start(f32[256]{0:T(256)} %param.11) | copy-start | bytes 3076

commit v5 on v4

--- a/solution.py
+++ b/solution.py
@@ -184,7 +184,7 @@
     base = slot * 128 + cols % ROWS
     late = (away == 2) | (other & (away != 0))
     place = jnp.where(away == 0, 0, jnp.where(away == 1, 2, 3)) + jnp.where(other, 1, 0)
-    place = jnp.where(late, jnp.where(away == 2, 4, jnp.where(away == 1, 5, 6)) + jnp.where(other, 1, 0), place)
+    place = jnp.where(late, 4 + jnp.where(other, jnp.where(away == 2, 3, jnp.where(away == 1, 1, 2)), 0), place)
     below, above, here = side == loop - 1, side == 1, side == 0
     kind = jnp.where(here, 4, jnp.where(above, 2, 0) + late.astype(jnp.int32))
     kind = jnp.where(below | above | here, kind, 5)
@@ -217,12 +217,13 @@
     ahead = lax.ppermute(one[:half], "rep", away[1])
     behind = lax.ppermute(three[half:], "rep", away[3])
     both = jnp.concatenate([one, three], axis=0)
-    sib_own = lax.ppermute(features, "rep", sibling)
+    spare, words = lax.optimization_barrier((features, words))
+    sib_own = lax.ppermute(spare, "rep", sibling)
     early = [features, sib_own, both]
     sums = aggregate([upper, lower], (0, 2), early, 8, 8)
     ahead, behind, *sums = lax.optimization_barrier((ahead, behind, *sums))
     two = jnp.concatenate([ahead, behind], axis=0)
-    late = [two, lax.ppermute(two, "rep", sibling), lax.ppermute(both, "rep", sibling)]
+    late = [two, lax.ppermute(jnp.concatenate([both, two], axis=0), "rep", sibling)]
     for_upper, for_lower = aggregate([upper, lower], (1, 3), late, 10, 4, sums, True)
     from_below = lax.ppermute(for_upper, "blk", up)
     from_above = lax.ppermute(for_lower, "blk", down)

time: 95.1 us -> 102 us (1.073)
  waiting for transfers between devices: 17.1 us -> 31.2 us
  starting transfers between devices: 55.3 us -> 48 us
    ppermute x1, waiting for transfers between devices: 4.84 us -> 15.1 us  [shards(): lower = lax.ppermute(words, 'blk', up)]
    ppermute x1, starting transfers between devices: 10.2 us -> 3.18 us  [shards(): from_above = lax.ppermute(for_lower, 'blk', down)]
    ppermute x3 -> x2, starting transfers between devices: 10.2 us -> 16.5 us  [the longest x1 8.35 us: shards(): lax.ppermute(jnp.concatenate([both, two], axis=0), 'rep', sibling)]
    ppermute x1, starting transfers between devices: 13.1 us -> 8.5 us  [shards(): upper = lax.ppermute(words, 'blk', down)]
    ppermute x1, waiting for transfers between devices: 0.86 us -> 5.45 us  [shards(): from_above = lax.ppermute(for_lower, 'blk', down)]
    ppermute x1, starting transfers between devices: 1.92 us -> 5.17 us  [shards(): three = lax.ppermute(features, 'rep', away[3])]
    ppermute x1, waiting for transfers between devices: 3.22 us -> 0.01 us  [shards(): behind = lax.ppermute(three[half:], 'rep', away[3])]
    ppermute x1, starting transfers between devices: 6.7 us -> 3.59 us  [shards(): one = lax.ppermute(features, 'rep', away[1])]
  transfers between devices with their start and end apart: 11 -> 10, of which waited for: 6 -> 5; matrix products, arithmetic and copies ran while one was open for 3% -> 4% of each run, Pallas kernels for 11% -> 10%
where the time goes in v5:
time: 102 us; the launch traced here: 101 us
  starting transfers between devices  48 us (47%)
  waiting for transfers between devices  31.2 us (31%)
  Pallas kernels  17.3 us (17%)
  other arithmetic  2.94 us (3%)
  local copies, waits for them, and re-layouts  1.03 us (1%)
    pallas_call x3, Pallas kernels, aggregate(): pl.pallas_call(functools.partial(aggregate_kernel, sources, kinds, width,...  15.6 us
    ppermute x1, waiting for transfers between devices, shards(): lower = lax.ppermute(words, 'blk', up)  15.1 us
    ppermute x1, starting transfers between devices, shards(): upper = lax.ppermute(words, 'blk', down)  8.5 us
    ppermute x1, starting transfers between devices, shards(): lax.ppermute(jnp.concatenate([both, two], axis=0), 'rep', sibling)  8.35 us
    ppermute x1, starting transfers between devices, shards(): sib_own = lax.ppermute(spare, 'rep', sibling)  8.11 us
    ppermute x1, waiting for transfers between devices, shards(): from_below = lax.ppermute(for_upper, 'blk', up)  7.51 us
    ppermute x1, waiting for transfers between devices, shards(): from_above = lax.ppermute(for_lower, 'blk', down)  5.45 us
    ppermute x1, starting transfers between devices, shards(): three = lax.ppermute(features, 'rep', away[3])  5.17 us
  transfers between devices with their start and end apart: 10, of which 5 were waited for; matrix products, arithmetic and copies ran while one was open for 4% of the time, Pallas kernels for 10%

profile of v5, /device:TPU:1, one launch (start us, length us, event | category | flops | bytes accessed | tf_op | source)
XLA Modules:
  0.0 100.8 jit_solution(9450986907903234949)
XLA Ops:
  0.0 0.0 copy-start
  0.0 5.2 %collective-permute-start.2 = (bf16[1024,256]{1,0:T(8,128)(2,1)}, bf16[1024,256]{1,0:T(8,128)(2,1)S(1)}, u32[]{:S(2)}, u32[]{:S(2)}) collective-permute-start(bf16[1024,256]{1,0:T(8,128)(2,1)} %features_ref.1), channel_id=1, source_target_pairs={{0,2},{1,3},{2,4},{3,5},{4,6},{5,7},{6,0},{7,1},{8,10},{9,11},{10,... | collective-permute-start | bytes 1572872 | tf_op jit(solution)/shard_map/ppermute | solution.py:210
  5.2 3.6 %collective-permute-start.1 = (bf16[1024,256]{1,0:T(8,128)(2,1)}, bf16[1024,256]{1,0:T(8,128)(2,1)S(1)}, u32[]{:S(2)}, u32[]{:S(2)}) collective-permute-start(bf16[1024,256]{1,0:T(8,128)(2,1)} %features_ref.1), channel_id=1, source_target_pairs={{0,6},{1,7},{2,0},{3,1},{4,2},{5,3},{6,4},{7,5},{8,14},{9,15},{10,... | collective-permute-start | bytes 1572872 | tf_op jit(solution)/shard_map/ppermute | solution.py:209
  8.8 0.8 copy.8
  9.6 0.1 fusion.10
  9.8 0.1 select_select_fusion
  9.8 0.1 copy.12
  9.9 0.9 convert_reduce_fusion
  10.8 0.3 add_reduce_fusion
  11.1 1.2 %convert.10 = s16[8,44,4,128]{3,2,1,0:T(4,128)(2,1)S(1)} convert(s32[8,44,4,128]{3,2,1,0:T(4,128)} %param.8) | non-fusion elementwise | flops 180224 | bytes 1081344 | tf_op jit(solution)/shard_map/convert.5
  12.4 0.0 copy-done
  12.4 8.1 %collective-permute-start = (bf16[1024,256]{1,0:T(8,128)(2,1)S(1)}, bf16[1024,256]{1,0:T(8,128)(2,1)S(1)}, u32[]{:S(2)}, u32[]{:S(2)}) collective-permute-start(bf16[1024,256]{1,0:T(8,128)(2,1)S(1)} %copy-done), channel_id=1, source_target_pairs={{0,1},{1,0},{2,3},{3,2},{4,5},{5,4},{6,7},{7,6},{8,9},{9,8},{10,11... | collective-permute-start | bytes 1572872 | tf_op jit(solution)/shard_map/ppermute | solution.py:221
  20.5 1.9 %collective-permute-start.6 = (s16[8,192,128]{2,1,0:T(8,128)(2,1)S(1)}, s16[8,192,128]{2,1,0:T(8,128)(2,1)S(1)}, u32[]{:S(2)}, u32[]{:S(2)}) collective-permute-start(s16[8,192,128]{2,1,0:T(8,128)(2,1)S(1)} %pad_add_fusion.refs_0_), channel_id=1, source_target_pairs={{0,8},{8,16},{16,24},{24,32},{32,40},{40,48},{48,56},{56,64},{64,7... | collective-permute-start | bytes 1179656 | tf_op jit(solution)/shard_map/ppermute | solution.py:215
  22.5 8.5 %collective-permute-start.5 = (s16[8,192,128]{2,1,0:T(8,128)(2,1)S(1)}, s16[8,192,128]{2,1,0:T(8,128)(2,1)S(1)}, u32[]{:S(2)}, u32[]{:S(2)}) collective-permute-start(s16[8,192,128]{2,1,0:T(8,128)(2,1)S(1)} %pad_add_fusion.refs_0_), channel_id=1, source_target_pairs={{8,0},{16,8},{24,16},{32,24},{40,32},{48,40},{56,48},{64,56},{72,6... | collective-permute-start | bytes 1179656 | tf_op jit(solution)/shard_map/ppermute | solution.py:214
  31.0 0.0 collective-permute-done.2
  31.0 3.0 %collective-permute-start.4 = (bf16[512,256]{1,0:T(8,128)(2,1)S(1)}, bf16[512,256]{1,0:T(8,128)(2,1)S(1)}, u32[]{:S(2)}, u32[]{:S(2)}) collective-permute-start(bf16[512,256]{1,0:T(8,128)(2,1)S(1)} %slice.9), channel_id=1, source_target_pairs={{0,2},{1,3},{2,4},{3,5},{4,6},{5,7},{6,0},{7,1},{8,10},{9,11},{10,... | collective-permute-start | bytes 786440 | tf_op jit(solution)/shard_map/ppermute | solution.py:218
  34.0 0.3 collective-permute-done.1
  34.4 4.1 %collective-permute-start.3 = (bf16[512,256]{1,0:T(8,128)(2,1)S(1)}, bf16[512,256]{1,0:T(8,128)(2,1)S(1)}, u32[]{:S(2)}, u32[]{:S(2)}) collective-permute-start(bf16[512,256]{1,0:T(8,128)(2,1)S(1)} %slice.8), channel_id=1, source_target_pairs={{0,6},{1,7},{2,0},{3,1},{4,2},{5,3},{6,4},{7,5},{8,14},{9,15},{10,... | collective-permute-start | bytes 786440 | tf_op jit(solution)/shard_map/ppermute | solution.py:217
  38.5 15.1 %collective-permute-done.6.refs_1_ = s16[8,192,128]{2,1,0:T(8,128)(2,1)S(1)} collective-permute-done((s16[8,192,128]{2,1,0:T(8,128)(2,1)S(1)}, s16[8,192,128]{2,1,0:T(8,128)(2,1)S(1)}, u32[]{:S(2)}, u32[]{:S(2)}) %collective-permute-start.6) | collective-permute-done | bytes 393248 | tf_op jit(solution)/shard_map/ppermute | solution.py:215
  53.7 0.0 collective-permute-done.5.refs_0_
  53.7 0.0 collective-permute-done.refs_3_.refs_2_
  53.7 5.6 %aggregate.3 = (f32[8,128,256]{2,1,0:T(8,128)S(1)}, f32[8,128,256]{2,1,0:T(8,128)S(1)}) custom-call(s16[8,192,128]{2,1,0:T(8,128)(2,1)S(1)} %collective-permute-done.5.refs_0_, s16[8,192,128]{2,1,0:T(8,128)(2,1)S(1)} %collective-permute-done.6.refs_1_, bf16[1024,256]{1,0:T(8,128)(2,1)S(1)} %copy-done, ...), custom_call_target="tpu_custom_call" | custom-call | tf_op jit(solution)/shard_map/aggregate/pallas_call | solution.py:127
  59.3 0.0 collective-permute-done.4
  59.3 0.0 collective-permute-done.3
  59.3 0.1 pad_maximum_fusion
  59.4 8.4 %collective-permute-start.7 = (bf16[3072,256]{1,0:T(8,128)(2,1)S(1)}, bf16[3072,256]{1,0:T(8,128)(2,1)S(1)}, u32[]{:S(2)}, u32[]{:S(2)}) collective-permute-start(bf16[3072,256]{1,0:T(8,128)(2,1)S(1)} %pad_maximum_fusion), channel_id=1, source_target_pairs={{0,1},{1,0},{2,3},{3,2},{4,5},{5,4},{6,7},{7,6},{8,9},{9,8},{10,11... | collective-permute-start | bytes 4718600 | tf_op jit(solution)/shard_map/ppermute | solution.py:226
  67.8 0.0 copy-start.4
  67.8 2.8 %collective-permute-done.7.refs_5_.refs_3_ = bf16[3072,256]{1,0:T(8,128)(2,1)S(1)} collective-permute-done((bf16[3072,256]{1,0:T(8,128)(2,1)S(1)}, bf16[3072,256]{1,0:T(8,128)(2,1)S(1)}, u32[]{:S(2)}, u32[]{:S(2)}) %collective-permute-start.7) | collective-permute-done | bytes 1572896 | tf_op jit(solution)/shard_map/ppermute | solution.py:226
  70.6 5.7 %aggregate.5 = (s16[1040,256]{1,0:T(8,128)(2,1)S(1)}, s16[1040,256]{1,0:T(8,128)(2,1)S(1)}) custom-call(s16[8,192,128]{2,1,0:T(8,128)(2,1)S(1)} %collective-permute-done.5.refs_0_, s16[8,192,128]{2,1,0:T(8,128)(2,1)S(1)} %collective-permute-done.6.refs_1_, bf16[1024,256]{1,0:T(8,128)(2,1)S(1)} %constant_dynamic-update-slice_fusion.2.refs_4_.refs_2_, ...), custom_call_target="tpu_custom_call" | custom-call | tf_op jit(solution)/shard_map/aggregate/pallas_call | solution.py:127
  76.4 3.2 %collective-permute-start.9 = (s16[1040,256]{1,0:T(8,128)(2,1)S(1)}, s16[1040,256]{1,0:T(8,128)(2,1)S(1)}, u32[]{:S(2)}, u32[]{:S(2)}) collective-permute-start(s16[1040,256]{1,0:T(8,128)(2,1)S(1)} %get-tuple-element.25), channel_id=1, source_target_pairs={{8,0},{16,8},{24,16},{32,24},{40,32},{48,40},{56,48},{64,56},{72,6... | collective-permute-start | bytes 1597448 | tf_op jit(solution)/shard_map/ppermute | solution.py:229
  79.5 2.1 %collective-permute-start.8 = (s16[1040,256]{1,0:T(8,128)(2,1)S(1)}, s16[1040,256]{1,0:T(8,128)(2,1)S(1)}, u32[]{:S(2)}, u32[]{:S(2)}) collective-permute-start(s16[1040,256]{1,0:T(8,128)(2,1)S(1)} %get-tuple-element.24), channel_id=1, source_target_pairs={{0,8},{8,16},{16,24},{24,32},{32,40},{40,48},{48,56},{56,64},{64,7... | collective-permute-start | bytes 1597448 | tf_op jit(solution)/shard_map/ppermute | solution.py:228
  81.7 0.0 copy-done.4
  81.7 0.2 and_reduce_fusion
  81.8 0.0 copy-start.1
  81.8 0.0 copy-start.2
  81.9 0.0 copy-start.3
  81.9 4.2 %aggregate.4.own_ref = f32[8,128,256]{2,1,0:T(8,128)S(1)} custom-call(s16[8,192,128]{2,1,0:T(8,128)(2,1)S(1)} %pad_add_fusion.refs_0_, bf16[1024,256]{1,0:T(8,128)(2,1)S(1)} %copy-done, bf16[1024,256]{1,0:T(8,128)(2,1)S(1)} %collective-permute-done.refs_3_.refs_2_, bf16[2048,256]{1,0:T(8,128)(2,1)S(1)} %constant_dynamic-update-slice_fusion.refs_4_.refs_3_, ...), custom_call_target="tpu_custom_call" | custom-call | tf_op jit(solution)/shard_map/aggregate/pallas_call | solution.py:127
  86.1 5.4 %collective-permute-done.9.down_ref = s16[1040,256]{1,0:T(8,128)(2,1)S(1)} collective-permute-done((s16[1040,256]{1,0:T(8,128)(2,1)S(1)}, s16[1040,256]{1,0:T(8,128)(2,1)S(1)}, u32[]{:S(2)}, u32[]{:S(2)}) %collective-permute-start.9) | collective-permute-done | bytes 532512 | tf_op jit(solution)/shard_map/ppermute | solution.py:229
  91.6 7.5 %collective-permute-done.8.up_ref = s16[1040,256]{1,0:T(8,128)(2,1)S(1)} collective-permute-done((s16[1040,256]{1,0:T(8,128)(2,1)S(1)}, s16[1040,256]{1,0:T(8,128)(2,1)S(1)}, u32[]{:S(2)}, u32[]{:S(2)}) %collective-permute-start.8) | collective-permute-done | bytes 532512 | tf_op jit(solution)/shard_map/ppermute | solution.py:228
  99.1 0.0 copy-done.1
  99.1 0.0 copy-done.2
  99.1 0.0 copy-done.3
  99.1 1.7 %finish.1 = bf16[1024,256]{1,0:T(8,128)(2,1)} custom-call(f32[8,128,256]{2,1,0:T(8,128)S(1)} %aggregate.4.own_ref, s16[1040,256]{1,0:T(8,128)(2,1)S(1)} %collective-permute-done.8.up_ref, s16[1040,256]{1,0:T(8,128)(2,1)S(1)} %collective-permute-done.9.down_ref, f32[8,128]{1,0:T(8,128)S(1)} %convert_element_type.16.degree_ref, bf16[1024,256]{1,0:T(8,128)(2,1)S(1)} %copy-done, ...), custom_call_target="tpu_custom_call" | custom-call | flops 268435456 | bytes 4194304 | tf_op jit(solution)/shard_map/finish/pallas_call | solution.py:165
  (15 shorter events, 0.2 us)
Async XLA Ops:
  0.0 12.4 %copy-start = (bf16[1024,256]{1,0:T(8,128)(2,1)S(1)}, bf16[1024,256]{1,0:T(8,128)(2,1)}, u32[]{:S(2)}) copy-start(bf16[1024,256]{1,0:T(8,128)(2,1)} %features_ref.1) | copy-start | bytes 1572868
  0.0 31.0 %collective-permute-start.2 = (bf16[1024,256]{1,0:T(8,128)(2,1)}, bf16[1024,256]{1,0:T(8,128)(2,1)S(1)}, u32[]{:S(2)}, u32[]{:S(2)}) collective-permute-start(bf16[1024,256]{1,0:T(8,128)(2,1)} %features_ref.1), channel_id=1, source_target_pairs={{0,2},{1,3},{2,4},{3,5},{4,6},{5,7},{6,0},{7,1},{8,10},{9,11},{10,... | collective-permute-start | bytes 1572872 | tf_op jit(solution)/shard_map/ppermute | solution.py:210
  5.2 29.2 %collective-permute-start.1 = (bf16[1024,256]{1,0:T(8,128)(2,1)}, bf16[1024,256]{1,0:T(8,128)(2,1)S(1)}, u32[]{:S(2)}, u32[]{:S(2)}) collective-permute-start(bf16[1024,256]{1,0:T(8,128)(2,1)} %features_ref.1), channel_id=1, source_target_pairs={{0,6},{1,7},{2,0},{3,1},{4,2},{5,3},{6,4},{7,5},{8,14},{9,15},{10,... | collective-permute-start | bytes 1572872 | tf_op jit(solution)/shard_map/ppermute | solution.py:209
  12.4 41.2 %collective-permute-start = (bf16[1024,256]{1,0:T(8,128)(2,1)S(1)}, bf16[1024,256]{1,0:T(8,128)(2,1)S(1)}, u32[]{:S(2)}, u32[]{:S(2)}) collective-permute-start(bf16[1024,256]{1,0:T(8,128)(2,1)S(1)} %copy-done), channel_id=1, source_target_pairs={{0,1},{1,0},{2,3},{3,2},{4,5},{5,4},{6,7},{7,6},{8,9},{9,8},{10,11... | collective-permute-start | bytes 1572872 | tf_op jit(solution)/shard_map/ppermute | solution.py:221
  20.5 33.1 %collective-permute-start.6 = (s16[8,192,128]{2,1,0:T(8,128)(2,1)S(1)}, s16[8,192,128]{2,1,0:T(8,128)(2,1)S(1)}, u32[]{:S(2)}, u32[]{:S(2)}) collective-permute-start(s16[8,192,128]{2,1,0:T(8,128)(2,1)S(1)} %pad_add_fusion.refs_0_), channel_id=1, source_target_pairs={{0,8},{8,16},{16,24},{24,32},{32,40},{40,48},{48,56},{56,64},{64,7... | collective-permute-start | bytes 1179656 | tf_op jit(solution)/shard_map/ppermute | solution.py:215
  22.5 31.2 %collective-permute-start.5 = (s16[8,192,128]{2,1,0:T(8,128)(2,1)S(1)}, s16[8,192,128]{2,1,0:T(8,128)(2,1)S(1)}, u32[]{:S(2)}, u32[]{:S(2)}) collective-permute-start(s16[8,192,128]{2,1,0:T(8,128)(2,1)S(1)} %pad_add_fusion.refs_0_), channel_id=1, source_target_pairs={{8,0},{16,8},{24,16},{32,24},{40,32},{48,40},{56,48},{64,56},{72,6... | collective-permute-start | bytes 1179656 | tf_op jit(solution)/shard_map/ppermute | solution.py:214
  31.0 28.3 %collective-permute-start.4 = (bf16[512,256]{1,0:T(8,128)(2,1)S(1)}, bf16[512,256]{1,0:T(8,128)(2,1)S(1)}, u32[]{:S(2)}, u32[]{:S(2)}) collective-permute-start(bf16[512,256]{1,0:T(8,128)(2,1)S(1)} %slice.9), channel_id=1, source_target_pairs={{0,2},{1,3},{2,4},{3,5},{4,6},{5,7},{6,0},{7,1},{8,10},{9,11},{10,... | collective-permute-start | bytes 786440 | tf_op jit(solution)/shard_map/ppermute | solution.py:218
  34.4 24.9 %collective-permute-start.3 = (bf16[512,256]{1,0:T(8,128)(2,1)S(1)}, bf16[512,256]{1,0:T(8,128)(2,1)S(1)}, u32[]{:S(2)}, u32[]{:S(2)}) collective-permute-start(bf16[512,256]{1,0:T(8,128)(2,1)S(1)} %slice.8), channel_id=1, source_target_pairs={{0,6},{1,7},{2,0},{3,1},{4,2},{5,3},{6,4},{7,5},{8,14},{9,15},{10,... | collective-permute-start | bytes 786440 | tf_op jit(solution)/shard_map/ppermute | solution.py:217
  59.4 11.2 %collective-permute-start.7 = (bf16[3072,256]{1,0:T(8,128)(2,1)S(1)}, bf16[3072,256]{1,0:T(8,128)(2,1)S(1)}, u32[]{:S(2)}, u32[]{:S(2)}) collective-permute-start(bf16[3072,256]{1,0:T(8,128)(2,1)S(1)} %pad_maximum_fusion), channel_id=1, source_target_pairs={{0,1},{1,0},{2,3},{3,2},{4,5},{5,4},{6,7},{7,6},{8,9},{9,8},{10,11... | collective-permute-start | bytes 4718600 | tf_op jit(solution)/shard_map/ppermute | solution.py:226
  67.8 13.8 %copy-start.4 = (s32[8,44,4,128]{3,2,1,0:T(4,128)S(1)}, s32[8,44,4,128]{3,2,1,0:T(4,128)}, u32[]{:S(2)}) copy-start(s32[8,44,4,128]{3,2,1,0:T(4,128)} %param.8) | copy-start | bytes 2162692
  76.4 15.2 %collective-permute-start.9 = (s16[1040,256]{1,0:T(8,128)(2,1)S(1)}, s16[1040,256]{1,0:T(8,128)(2,1)S(1)}, u32[]{:S(2)}, u32[]{:S(2)}) collective-permute-start(s16[1040,256]{1,0:T(8,128)(2,1)S(1)} %get-tuple-element.25), channel_id=1, source_target_pairs={{8,0},{16,8},{24,16},{32,24},{40,32},{48,40},{56,48},{64,56},{72,6... | collective-permute-start | bytes 1597448 | tf_op jit(solution)/shard_map/ppermute | solution.py:229
  79.5 19.5 %collective-permute-start.8 = (s16[1040,256]{1,0:T(8,128)(2,1)S(1)}, s16[1040,256]{1,0:T(8,128)(2,1)S(1)}, u32[]{:S(2)}, u32[]{:S(2)}) collective-permute-start(s16[1040,256]{1,0:T(8,128)(2,1)S(1)} %get-tuple-element.24), channel_id=1, source_target_pairs={{0,8},{8,16},{16,24},{24,32},{32,40},{40,48},{48,56},{56,64},{64,7... | collective-permute-start | bytes 1597448 | tf_op jit(solution)/shard_map/ppermute | solution.py:228
  81.8 17.2 %copy-start.1 = (bf16[256,256]{1,0:T(8,128)(2,1)S(1)}, bf16[256,256]{1,0:T(8,128)(2,1)}, u32[]{:S(2)}) copy-start(bf16[256,256]{1,0:T(8,128)(2,1)} %self_ref.1) | copy-start | bytes 393220
  81.8 17.2 %copy-start.2 = (bf16[256,256]{1,0:T(8,128)(2,1)S(1)}, bf16[256,256]{1,0:T(8,128)(2,1)}, u32[]{:S(2)}) copy-start(bf16[256,256]{1,0:T(8,128)(2,1)} %neigh_ref.1) | copy-start | bytes 393220
  81.9 17.2 %copy-start.3 = (f32[256]{0:T(256)S(1)}, f32[256]{0:T(256)}, u32[]{:S(2)}) copy-start(f32[256]{0:T(256)} %param.11) | copy-start | bytes 3076
